TPU v7x, 256 devices: a whole 4x4x8 slice. The times are simulated.
256 devices in a mesh: dp: 32 (over x, z), tile: 8 (over y, core).
Axes of the slice: x: 4, y: 4, z: 8, core: 2. Of those that a mesh axis runs over, the one named last changes fastest.
Arguments:
- queries: bfloat16 [16384, 768], P('dp'), may hold values from -30 to 30
- passages: bfloat16 [262144, 768], P(('dp', 'tile')), may hold values from -30 to 30
- query_cluster: int32 [16384], P('dp'), may hold values from 0 to 127, as said below
- passage_cluster: int32 [262144], P(('dp', 'tile')), may hold values from 0 to 127, as said below
- positive: int32 [16384], P('dp'), may hold values from 0 to 262143, as said below
Outputs:
- query_grad: bfloat16 [16384, 768], P('dp')
- passage_grad: bfloat16 [262144, 768], P(('dp', 'tile'))
Inputs may be any that keep to these rules, and one draw needn't show every extreme that they name: `query_cluster`: among the 512 queries of one dp index, at most 32 have clusters of one owner o (clusters o * 4 to o * 4 + 3), and in every draw some owner receives exactly 32 of them. `passage_cluster`: the passages on dp index d belong to clusters d * 4 to d * 4 + 3; every cluster has a passage. passage_cluster[positive[i]] == query_cluster[i].
All inputs are finite; a program needn't handle non-finite values.
Results may differ from a plain program's by a relative error of at most 0.015.
Values may be sent and summed in bfloat16 or wider, within the bound.
A program may use at most 64 MiB of HBM per device.

v0:
```python
import math

import jax
import jax.numpy as jnp
from jax import lax
from jax.sharding import PartitionSpec as P

CL_OWN = 4


NEGATIVE = -1e30
SOFTMAX_TEMP = 2.0


def prefix_ends(width):
    twelfth = width // 12
    return [twelfth, 2 * twelfth, 4 * twelfth, 8 * twelfth, width]


def contract(left, right):
    return lax.dot_general(
        left, right, (((1,), (1,)), ((), ())), preferred_element_type=jnp.float32
    )


def prefix_logits(query_block, passages, prefix_limits):
    scaled_scores = []
    for final_column in prefix_limits:
        scaled_scores.append(
            contract(query_block[:, :final_column], passages[:, :final_column])
            * (SOFTMAX_TEMP / math.sqrt(final_column))
        )
    return scaled_scores


def body(queries, passages, query_cluster, passage_cluster, positive):
    width = queries.shape[1]
    prefix_limits = prefix_ends(width)
    starts = [0] + prefix_limits[:-1]
    query_total = queries.shape[0]
    passage_total = passages.shape[0]
    dp_count = lax.axis_size("dp")
    tile_count = lax.axis_size("tile")
    capacity = 2 * query_total // dp_count
    slot_total = dp_count * capacity
    owners = query_cluster // CL_OWN
    owner_onehot = (owners[:, None] == jnp.arange(dp_count, dtype=jnp.int32)[None, :]).astype(
        jnp.int32
    )
    ranks = jnp.sum((jnp.cumsum(owner_onehot, axis=0) - 1) * owner_onehot, axis=1)
    slots = owners * capacity + ranks
    send_rows = jnp.zeros((slot_total, width), jnp.bfloat16).at[slots].set(queries)
    send_clusters = jnp.full((slot_total,), -1, jnp.int32).at[slots].set(query_cluster)
    send_targets = jnp.full((slot_total,), -1, jnp.int32).at[slots].set(positive)
    arrived, arrived_clusters, arrived_targets = (
        lax.all_to_all(send_rows, "dp", split_axis=0, concat_axis=0, tiled=True),
        lax.all_to_all(send_clusters, "dp", split_axis=0, concat_axis=0, tiled=True),
        lax.all_to_all(send_targets, "dp", split_axis=0, concat_axis=0, tiled=True),
    )
    first_row = (lax.axis_index("dp") * tile_count + lax.axis_index("tile")) * passage_total
    local_targets = arrived_targets - first_row
    block_rows = math.gcd(slot_total, 512)
    block_count = slot_total // block_rows
    row_blocks = arrived.reshape(block_count, block_rows, width)
    cluster_blocks = arrived_clusters.reshape(block_count, block_rows)
    target_blocks = local_targets.reshape(block_count, block_rows)
    column_ids = jnp.arange(passage_total, dtype=jnp.int32)

    def first_pass(items):
        query_block, clusters = items
        member = clusters[:, None] == passage_cluster[None, :]
        scaled_scores = prefix_logits(query_block, passages, prefix_limits)
        highest_list = []
        total_list = []
        for value in scaled_scores:
            highest = jnp.max(jnp.where(member, value, NEGATIVE), axis=1)
            highest_list.append(highest)
            total_list.append(
                jnp.sum(jnp.where(member, jnp.exp(value - highest[:, None]), 0.0), axis=1)
            )
        return (jnp.stack(highest_list), jnp.stack(total_list))

    local_highest, local_totals = lax.map(first_pass, (row_blocks, cluster_blocks))
    global_highest = lax.pmax(local_highest, "tile")
    global_totals = lax.psum(local_totals * jnp.exp(local_highest - global_highest), "tile")
    log_totals = global_highest + jnp.log(jnp.where(global_totals > 0, global_totals, 1.0))

    def second_pass(carry, items):
        query_block, clusters, targets, block_log_totals = items
        member = clusters[:, None] == passage_cluster[None, :]
        target_indicator = (targets[:, None] == column_ids[None, :]).astype(jnp.float32)
        scaled_scores = prefix_logits(query_block, passages, prefix_limits)
        weights = [None] * len(prefix_limits)
        running = None
        for target_position in reversed(range(len(prefix_limits))):
            probabilities = jnp.where(
                member,
                jnp.exp(
                    scaled_scores[target_position] - block_log_totals[target_position][:, None]
                ),
                0.0,
            )
            logit_delta = (probabilities - target_indicator) * (
                SOFTMAX_TEMP / math.sqrt(prefix_limits[target_position])
            )
            running = logit_delta if running is None else running + logit_delta
            weights[target_position] = running.astype(jnp.bfloat16)
        query_parts = []
        passage_parts = []
        for target_position in range(len(prefix_limits)):
            start_col = starts[target_position]
            final_column = prefix_limits[target_position]
            query_parts.append(
                jnp.dot(
                    weights[target_position],
                    passages[:, start_col:final_column],
                    preferred_element_type=jnp.float32,
                )
            )
            passage_parts.append(
                lax.dot_general(
                    weights[target_position],
                    query_block[:, start_col:final_column],
                    (((0,), (0,)), ((), ())),
                    preferred_element_type=jnp.float32,
                )
            )
        return (
            carry + jnp.concatenate(passage_parts, axis=1),
            jnp.concatenate(query_parts, axis=1),
        )

    passage_init = jnp.zeros((passage_total, width), jnp.float32)
    passage_sum, query_partial = lax.scan(
        second_pass, passage_init, (row_blocks, cluster_blocks, target_blocks, log_totals)
    )
    query_partial = query_partial.reshape(slot_total, width)
    summed = lax.psum(query_partial.astype(jnp.bfloat16), "tile")
    returned = lax.all_to_all(summed, "dp", split_axis=0, concat_axis=0, tiled=True)
    query_grad = returned[slots]
    return (query_grad, passage_sum.astype(jnp.bfloat16))


def solution(mesh):
    in_specs = (P("dp", None), P(("dp", "tile"), None), P("dp"), P(("dp", "tile")), P("dp"))
    out_specs = (P("dp", None), P(("dp", "tile"), None))
    return jax.shard_map(body, mesh=mesh, in_specs=in_specs, out_specs=out_specs, check_vma=False)
```

profile of v0, /device:TPU:1, one launch (start us, length us, event | category | flops | bytes accessed | tf_op | source)
XLA Modules:
  0.0 339.4 jit_solution(11619695298797105366)
XLA Ops:
  10.8 2.6 scatter_custom_fusion
  14.1 11.9 %all-to-all-start = ((s32[32,32,1]{1,2,0:T(1,128)}), s32[32,32,1]{1,2,0:T(1,128)S(1)}, u32[]{:S(2)}, u32[]{:S(2)}) async-start(s32[32,32,1]{1,2,0:T(1,128)} %all_to_all.26), calls=%async_computation | async-start | bytes 32768 | tf_op jit(solution)/shard_map/all_to_all | solution.py:57
  26.0 2.6 scatter_custom_fusion.2
  29.3 5.3 %all-to-all-done = s32[32,32,1]{1,2,0:T(1,128)S(1)} async-done(((s32[32,32,1]{1,2,0:T(1,128)}), s32[32,32,1]{1,2,0:T(1,128)S(1)}, u32[]{:S(2)}, u32[]{:S(2)}) %all-to-all-start) | async-done | bytes 4128 | tf_op jit(solution)/shard_map/all_to_all | solution.py:57
  34.5 4.0 %all-to-all-start.2 = ((s32[32,32,1]{1,2,0:T(1,128)}), s32[32,32,1]{1,2,0:T(1,128)S(1)}, u32[]{:S(2)}, u32[]{:S(2)}) async-start(s32[32,32,1]{1,2,0:T(1,128)} %all_to_all.30), calls=%async_computation.2 | async-start | bytes 32768 | tf_op jit(solution)/shard_map/all_to_all | solution.py:58
  38.5 4.5 %scatter_custom_fusion.1 = bf16[1024,768]{1,0:T(8,128)(2,1)} fusion(s32[512]{0:T(512)S(1)} %compare_select_fusion.16, bf16[512,768]{1,0:T(8,128)(2,1)} %param.9, bf16[]{:T(256)} %constant.89.clone.1), kind=kCustom, calls=%fused_computation.108 | custom fusion | bytes 1573376 | tf_op jit(solution)/shard_map/scatter | solution.py:52
  43.0 4.1 %all-to-all-done.2 = s32[32,32,1]{1,2,0:T(1,128)S(1)} async-done(((s32[32,32,1]{1,2,0:T(1,128)}), s32[32,32,1]{1,2,0:T(1,128)S(1)}, u32[]{:S(2)}, u32[]{:S(2)}) %all-to-all-start.2) | async-done | bytes 4128 | tf_op jit(solution)/shard_map/all_to_all | solution.py:58
  47.1 5.2 %all-to-all-start.1 = ((bf16[32,32,768]{2,1,0:T(8,128)(2,1)}), bf16[32,32,768]{2,1,0:T(8,128)(2,1)S(1)}, u32[]{:S(2)}, u32[]{:S(2)}) async-start(bf16[32,32,768]{2,1,0:T(8,128)(2,1)} %bitcast.113), calls=%async_computation.1 | async-start | bytes 3145728 | tf_op jit(solution)/shard_map/all_to_all | solution.py:56
  53.8 35.7 %all-to-all-done.1 = bf16[32,32,768]{2,1,0:T(8,128)(2,1)S(1)} async-done(((bf16[32,32,768]{2,1,0:T(8,128)(2,1)}), bf16[32,32,768]{2,1,0:T(8,128)(2,1)S(1)}, u32[]{:S(2)}, u32[]{:S(2)}) %all-to-all-start.1) | async-done | bytes 1572896 | tf_op jit(solution)/shard_map/all_to_all | solution.py:56
  89.6 24.0 %while.25 = (s32[]{:T(128)}, f32[2,5,512]{2,1,0:T(8,128)S(1)}, f32[2,5,512]{2,1,0:T(8,128)S(1)}, s32[2,512]{1,0:T(2,128)S(1)}, s32[1024]{0:T(1024)S(1)}, /*index...) while((s32[]{:T(128)}, f32[2,5,512]{2,1,0:T(8,128)S(1)}, ...), condition=%wide.region_17.18_spmd, body=%wide.region_6.17_spmd.sunk | while | flops 1831332864 | bytes 70146248 | solution.py:83
  92.4 3.4 %fusion.145 = (f32[512]{0:T(512)S(1)}, f32[512]{0:T(512)S(1)}, f32[512]{0:T(512)S(1)}, f32[512]{0:T(512)S(1)}, f32[512]{0:T(512)S(1)}, /*index=5*/f32[512,1024]{1,0:T(8,128)}) fusion(s32[1024]{0:T(1024)S(1)} %get-tuple-element.339, s32[512]{0:T(512)S(1)} %bitcast.115, f32[512,1024]{1,0:T(8,128)S(1)} %fusion.141, f32[512,1024]{1,0:T(8,128)S(1)} %fusion.142, ...), kind=kOutput, calls=%fused_computation.19.clone.1 | convolution fusion | flops 813692416 | bytes 12861440 | tf_op jit(solution)/shard_map/while/body/eval_jaxpr/dot_general | solution.py:21
  95.9 5.7 %fusion.146 = (f32[512]{0:T(512)S(1)}, f32[512]{0:T(512)S(1)}, f32[512]{0:T(512)S(1)}, f32[512]{0:T(512)S(1)}, f32[512]{0:T(512)S(1)}) fusion(f32[512,1024]{1,0:T(8,128)} %get-tuple-element.290, f32[512]{0:T(512)S(1)} %get-tuple-element.291, s32[1024]{0:T(1024)S(1)} %get-tuple-element.339, s32[512]{0:T(512)S(1)} %bitcast.116, ...), kind=kLoop, calls=%fused_computation.24.clone.1 | loop fusion | flops 11007488 | bytes 10512384 | tf_op jit(solution)/shard_map/while/body/eval_jaxpr/reduce_sum | solution.py:79
  104.4 3.4 %fusion.145 = (f32[512]{0:T(512)S(1)}, f32[512]{0:T(512)S(1)}, f32[512]{0:T(512)S(1)}, f32[512]{0:T(512)S(1)}, f32[512]{0:T(512)S(1)}, /*index=5*/f32[512,1024]{1,0:T(8,128)}) fusion(s32[1024]{0:T(1024)S(1)} %get-tuple-element.339, s32[512]{0:T(512)S(1)} %bitcast.115, f32[512,1024]{1,0:T(8,128)S(1)} %fusion.141, f32[512,1024]{1,0:T(8,128)S(1)} %fusion.142, ...), kind=kOutput, calls=%fused_computation.19.clone.1 | convolution fusion | flops 813692416 | bytes 12861440 | tf_op jit(solution)/shard_map/while/body/eval_jaxpr/dot_general | solution.py:21
  107.8 5.7 %fusion.146 = (f32[512]{0:T(512)S(1)}, f32[512]{0:T(512)S(1)}, f32[512]{0:T(512)S(1)}, f32[512]{0:T(512)S(1)}, f32[512]{0:T(512)S(1)}) fusion(f32[512,1024]{1,0:T(8,128)} %get-tuple-element.290, f32[512]{0:T(512)S(1)} %get-tuple-element.291, s32[1024]{0:T(1024)S(1)} %get-tuple-element.339, s32[512]{0:T(512)S(1)} %bitcast.116, ...), kind=kLoop, calls=%fused_computation.24.clone.1 | loop fusion | flops 11007488 | bytes 10512384 | tf_op jit(solution)/shard_map/while/body/eval_jaxpr/reduce_sum | solution.py:79
  113.6 23.4 %pmax.7 = f32[2,5,512]{2,1,0:T(8,128)S(1)} all-reduce(f32[2,5,512]{2,1,0:T(8,128)S(1)} %get-tuple-element.93), channel_id=1, replica_groups=mesh['dp'=32,'tile'=8] {'tile'}, use_global_device_ids=true, to_apply=%region_18.19 | all-reduce | flops 5120 | bytes 40960 | tf_op jit(solution)/shard_map/pmax | solution.py:84
  136.9 23.8 %psum.14 = f32[2,5,512]{2,1,0:T(8,128)S(1)} all-reduce(f32[2,5,512]{2,1,0:T(8,128)S(1)} %exponential_multiply_fusion), channel_id=1, replica_groups=mesh['dp'=32,'tile'=8] {'tile'}, use_global_device_ids=true, to_apply=%region_19.20 | all-reduce | flops 5120 | bytes 40960 | tf_op jit(solution)/shard_map/psum | solution.py:85
  160.8 56.0 %while.26 = (s32[]{:T(128)}, f32[1024,768]{0,1:T(8,128)}, bf16[2,512,768]{2,1,0:T(8,128)(2,1)}, s32[2,512]{1,0:T(2,128)S(1)}, s32[1024]{0:T(1024)S(1)}, /*index=...) while((s32[]{:T(128)}, f32[1024,768]{0,1:T(8,128)}, ...), condition=%wide.region_21.22_spmd.clone, body=%wide.region_20.21_spmd.clone.sunk | while | flops 3451912192 | bytes 146750512 | solution.py:134
  172.3 2.3 copy.19
  174.6 2.2 constant_dynamic-update-slice_fusion.2
  180.2 1.5 convolution_dynamic-update-slice_fusion.23
  182.1 1.5 convolution_dynamic-update-slice_fusion.24
  183.6 4.7 %select_add_fusion.2 = f32[1024,768]{0,1:T(8,128)} fusion(f32[1024,768]{0,1:T(8,128)} %convolution_dynamic-update-slice_fusion.24, f32[1024,768]{0,1:T(8,128)} %get-tuple-element.359, pred[]{:T(512)S(6)} %compare.5), kind=kLoop, calls=%fused_computation.51.clone.1 | loop fusion | flops 1572864 | bytes 9437185 | tf_op jit(solution)/shard_map/while/body/eval_jaxpr/add | solution.py:129
  199.8 2.3 copy.19
  202.1 2.2 constant_dynamic-update-slice_fusion.2
  207.7 1.5 convolution_dynamic-update-slice_fusion.23
  209.6 1.5 convolution_dynamic-update-slice_fusion.24
  211.1 5.6 %select_add_fusion.2 = f32[1024,768]{0,1:T(8,128)} fusion(f32[1024,768]{0,1:T(8,128)} %convolution_dynamic-update-slice_fusion.24, f32[1024,768]{0,1:T(8,128)} %get-tuple-element.359, pred[]{:T(512)S(6)} %compare.5), kind=kLoop, calls=%fused_computation.51.clone.1 | loop fusion | flops 1572864 | bytes 9437185 | tf_op jit(solution)/shard_map/while/body/eval_jaxpr/add | solution.py:129
  216.8 65.1 %all-reduce.2.cloned.1.call-done = bf16[32,32,768]{2,1,0:T(8,128)(2,1)} async-done(((bf16[32,32,768]{2,1,0:T(8,128)(2,1)}), bf16[32,32,768]{2,1,0:T(8,128)(2,1)}) %all-reduce.2.cloned.1.call-update) | async-done | bytes 1572880 | tf_op jit(solution)/shard_map/psum | solution.py:138
  281.9 9.7 %all-to-all-start.3 = ((bf16[32,32,768]{2,1,0:T(8,128)(2,1)}), bf16[32,32,768]{2,1,0:T(8,128)(2,1)}, u32[]{:S(2)}, u32[]{:S(2)}) async-start(bf16[32,32,768]{2,1,0:T(8,128)(2,1)} %all-reduce.2.cloned.1.call-done), calls=%async_computation.3 | async-start | bytes 3145728 | tf_op jit(solution)/shard_map/all_to_all | solution.py:139
  291.6 1.7 copy.13
  293.3 34.6 %all-to-all-done.3 = bf16[32,32,768]{2,1,0:T(8,128)(2,1)} async-done(((bf16[32,32,768]{2,1,0:T(8,128)(2,1)}), bf16[32,32,768]{2,1,0:T(8,128)(2,1)}, u32[]{:S(2)}, u32[]{:S(2)}) %all-to-all-start.3) | async-done | bytes 1572896 | tf_op jit(solution)/shard_map/all_to_all | solution.py:139
  327.9 4.7 %gather_fusion = bf16[512,768]{1,0:T(8,128)(2,1)} fusion(bf16[1024,768]{1,0:T(8,128)(2,1)} %bitcast.19, s32[1024]{0:T(1024)S(1)} %pad_clamp_fusion), kind=kCustom, calls=%fused_computation | custom fusion | bytes 1574912 | tf_op jit(solution)/shard_map/gather | solution.py:140
  (145 shorter events, 42.6 us)
Async XLA Ops:
  10.8 36.3 %copy-start.18 = (s32[512]{0:T(512)}, s32[512]{0:T(512)S(1)}, u32[]{:S(2)}) copy-start(s32[512]{0:T(512)S(1)} %compare_select_fusion.16) | copy-start | bytes 6148
  14.1 20.4 %all-to-all-start = ((s32[32,32,1]{1,2,0:T(1,128)}), s32[32,32,1]{1,2,0:T(1,128)S(1)}, u32[]{:S(2)}, u32[]{:S(2)}) async-start(s32[32,32,1]{1,2,0:T(1,128)} %all_to_all.26), calls=%async_computation | async-start | bytes 32768 | tf_op jit(solution)/shard_map/all_to_all | solution.py:57
  34.5 12.5 %all-to-all-start.2 = ((s32[32,32,1]{1,2,0:T(1,128)}), s32[32,32,1]{1,2,0:T(1,128)S(1)}, u32[]{:S(2)}, u32[]{:S(2)}) async-start(s32[32,32,1]{1,2,0:T(1,128)} %all_to_all.30), calls=%async_computation.2 | async-start | bytes 32768 | tf_op jit(solution)/shard_map/all_to_all | solution.py:58
  38.5 51.0 %copy-start = (bf16[1024,768]{1,0:T(8,128)(2,1)S(1)}, bf16[1024,768]{1,0:T(8,128)(2,1)}, u32[]{:S(2)}) copy-start(bf16[1024,768]{1,0:T(8,128)(2,1)} %param.10) | copy-start | bytes 4718596
  38.5 51.0 %copy-start.17 = (s32[1024]{0:T(1024)S(1)}, s32[1024]{0:T(1024)}, u32[]{:S(2)}) copy-start(s32[1024]{0:T(1024)} %param.12) | copy-start | bytes 12292
  47.1 42.5 %all-to-all-start.1 = ((bf16[32,32,768]{2,1,0:T(8,128)(2,1)}), bf16[32,32,768]{2,1,0:T(8,128)(2,1)S(1)}, u32[]{:S(2)}, u32[]{:S(2)}) async-start(bf16[32,32,768]{2,1,0:T(8,128)(2,1)} %bitcast.113), calls=%async_computation.1 | async-start | bytes 3145728 | tf_op jit(solution)/shard_map/all_to_all | solution.py:56
  52.2 229.7 %all-reduce.2.cloned.1.call-start = ((), (), s32[]{:S(2)}) async-start(), calls=%async_computation.4 | async-start | bytes 3145728 | tf_op jit(solution)/shard_map/psum | solution.py:138
  90.9 1.5 copy-start.2
  91.3 4.5 %copy-start.3 = (f32[512,1024]{1,0:T(8,128)}, f32[512,1024]{1,0:T(8,128)S(1)}, u32[]{:S(2)}) copy-start(f32[512,1024]{1,0:T(8,128)S(1)} %fusion.143) | copy-start | bytes 6291460 | tf_op jit(solution)/shard_map/while
  91.8 4.0 %copy-start.4 = (f32[512,1024]{1,0:T(8,128)}, f32[512,1024]{1,0:T(8,128)S(1)}, u32[]{:S(2)}) copy-start(f32[512,1024]{1,0:T(8,128)S(1)} %fusion.144) | copy-start | bytes 6291460 | tf_op jit(solution)/shard_map/while
  102.9 1.5 copy-start.2
  103.3 4.5 %copy-start.3 = (f32[512,1024]{1,0:T(8,128)}, f32[512,1024]{1,0:T(8,128)S(1)}, u32[]{:S(2)}) copy-start(f32[512,1024]{1,0:T(8,128)S(1)} %fusion.143) | copy-start | bytes 6291460 | tf_op jit(solution)/shard_map/while
  103.8 4.0 %copy-start.4 = (f32[512,1024]{1,0:T(8,128)}, f32[512,1024]{1,0:T(8,128)S(1)}, u32[]{:S(2)}) copy-start(f32[512,1024]{1,0:T(8,128)S(1)} %fusion.144) | copy-start | bytes 6291460 | tf_op jit(solution)/shard_map/while
  164.6 6.3 %copy-start.9 = (f32[512,1024]{1,0:T(8,128)}, f32[512,1024]{1,0:T(8,128)S(1)}, u32[]{:S(2)}) copy-start(f32[512,1024]{1,0:T(8,128)S(1)} %fusion.177) | copy-start | bytes 6291460 | tf_op jit(solution)/shard_map/while
  165.8 4.6 %copy-start.11 = (f32[512,1024]{1,0:T(8,128)}, f32[512,1024]{1,0:T(8,128)S(1)}, u32[]{:S(2)}) copy-start(f32[512,1024]{1,0:T(8,128)S(1)} %fusion.178) | copy-start | bytes 6291460 | tf_op jit(solution)/shard_map/while
  166.9 3.0 copy-start.5
  174.6 3.3 copy-start.8
  176.8 2.2 copy-start.6
  177.9 2.3 copy-start.12
  180.2 1.9 copy-start.10
  183.6 4.7 %copy-start.15 = (bf16[2,512,768]{2,1,0:T(8,128)(2,1)S(1)}, bf16[2,512,768]{2,1,0:T(8,128)(2,1)}, u32[]{:S(2)}) copy-start(bf16[2,512,768]{2,1,0:T(8,128)(2,1)} %copy-done.14) | copy-start | bytes 4718596 | tf_op jit(solution)/shard_map/while
  192.1 6.3 %copy-start.9 = (f32[512,1024]{1,0:T(8,128)}, f32[512,1024]{1,0:T(8,128)S(1)}, u32[]{:S(2)}) copy-start(f32[512,1024]{1,0:T(8,128)S(1)} %fusion.177) | copy-start | bytes 6291460 | tf_op jit(solution)/shard_map/while
  193.3 4.6 %copy-start.11 = (f32[512,1024]{1,0:T(8,128)}, f32[512,1024]{1,0:T(8,128)S(1)}, u32[]{:S(2)}) copy-start(f32[512,1024]{1,0:T(8,128)S(1)} %fusion.178) | copy-start | bytes 6291460 | tf_op jit(solution)/shard_map/while
  194.4 3.0 copy-start.5
  202.1 3.3 copy-start.8
  204.3 2.2 copy-start.6
  205.4 2.3 copy-start.12
  207.7 1.9 copy-start.10
  211.1 5.6 %copy-start.15 = (bf16[2,512,768]{2,1,0:T(8,128)(2,1)S(1)}, bf16[2,512,768]{2,1,0:T(8,128)(2,1)}, u32[]{:S(2)}) copy-start(bf16[2,512,768]{2,1,0:T(8,128)(2,1)} %copy-done.14) | copy-start | bytes 4718596 | tf_op jit(solution)/shard_map/while
  216.7 74.8 %copy-start.19 = (s32[512]{0:T(512)S(1)}, s32[512]{0:T(512)}, u32[]{:S(2)}) copy-start(s32[512]{0:T(512)} %copy-done.18) | copy-start | bytes 6148
  216.7 74.9 %copy-start.13 = (f32[1024,768]{0,1:T(8,128)S(1)}, f32[1024,768]{0,1:T(8,128)}, u32[]{:S(2)}) copy-start(f32[1024,768]{0,1:T(8,128)} %get-tuple-element.96) | copy-start | bytes 9437188
  281.9 46.0 %all-to-all-start.3 = ((bf16[32,32,768]{2,1,0:T(8,128)(2,1)}), bf16[32,32,768]{2,1,0:T(8,128)(2,1)}, u32[]{:S(2)}, u32[]{:S(2)}) async-start(bf16[32,32,768]{2,1,0:T(8,128)(2,1)} %all-reduce.2.cloned.1.call-done), calls=%async_computation.3 | async-start | bytes 3145728 | tf_op jit(solution)/shard_map/all_to_all | solution.py:139
  (8 other events, 9.9 us)
Sparse Core Ops, SparseCore 0:
  216.9 64.9 all-reduce.1
where the time goes:
time: 343 us; the launch traced here: 339 us
  waiting for transfers between devices  145 us (42%)
  blocking collectives  47.2 us (14%)
  matrix products  39.8 us (12%)
  local copies, waits for them, and re-layouts  36.3 us (11%)
  starting transfers between devices  30.9 us (9%)
  other arithmetic  25.7 us (7%)
  between operations  14.2 us (4%)
    psum x1, waiting for transfers between devices, body(): summed = lax.psum(query_partial.astype(jnp.bfloat16), 'tile')  65.1 us
    all_to_all x1, waiting for transfers between devices, body(): lax.all_to_all(send_rows, 'dp', split_axis=0, concat_axis=0, tiled=True)  35.7 us
    all_to_all x1, waiting for transfers between devices, body(): lax.all_to_all(summed, 'dp', split_axis=0, concat_axis=0, tiled=True)  34.6 us
    psum x1, blocking collectives, body(): lax.psum(local_totals * jnp.exp(local_highest - global_highest), 'tile')  23.8 us
    pmax x1, blocking collectives, body(): global_highest = lax.pmax(local_highest, 'tile')  23.4 us
    dot_general x20, matrix products, contract(): lax.dot_general(left, right, (((1,), (1,)), ((), ())), preferred_element_...  22.3 us
    dot_general x10, matrix products, second_pass(): lax.dot_general(weights[target_position], query_block[:, start_col:final_...  12.6 us
    all_to_all x1, starting transfers between devices, body(): lax.all_to_all(send_clusters, 'dp', split_axis=0, concat_axis=0, tiled=True)  11.9 us
  transfers between devices with their start and end apart: 5, of which 5 were waited for; matrix products, arithmetic and copies ran while one was open for 3% of the time, Pallas kernels for 0%

commit v1 on v0

v1 whole, which is shorter than its diff:
```python
import functools
import math

import jax
import jax.numpy as jnp
from jax import lax
from jax.experimental import pallas as pl
from jax.experimental.pallas import tpu as pltpu
from jax.sharding import PartitionSpec as P

F32 = jnp.float32
BF16 = jnp.bfloat16
I32 = jnp.int32

NX, NZ, NY, NC = 4, 8, 4, 2
CL_OWN = 4
CAP = 32
NEGATIVE = -1e30
CUTS = (64, 128, 256, 512, 768)
WIDTH = 768
META = 128
ROW = WIDTH + META
SCALES = tuple(2.0 / math.sqrt(k) for k in CUTS)
LOG2E = math.log2(math.e)
BLOCK = 128
PAIR = 2 * BLOCK
SLOTS = 8 * BLOCK
HALF = WIDTH // 2

PLACE = ((0, 0), (0, 1), (1, 0), (3, 0), (1, 1), (3, 1), (2, 0), (2, 1))
MIRROR = tuple(PLACE.index(((NY - dy) % NY, dc)) for dy, dc in PLACE)


def nn(a, b):
    return lax.dot_general(a, b, (((1,), (0,)), ((), ())), preferred_element_type=F32)


def nt(a, b):
    return lax.dot_general(a, b, (((1,), (1,)), ((), ())), preferred_element_type=F32)


def iota(shape, dim):
    return lax.broadcasted_iota(I32, shape, dim)


def onehot(mask):
    return jnp.where(mask, 1.0, 0.0).astype(BF16)


def fold(value, op):
    return op(value.reshape(value.shape[0] // 8, 8, value.shape[1]), axis=0)


def kernel(qc_ref, pos_ref, pc_ref, q_ref, p_hbm, qg_ref, pg_hbm,
           p_ref, p0_ref, p1_ref, pt_ref, xs, xr, zs, agb, q0_ref,
           prob, wt, msc, stat, stat_in, lse_ref, gt, sib, comb, half_in, from_m, from_p,
           zbs, zb, xbs, xb, fg, bsel_ref, fsel_ref, pg_ref,
           ssem, rsem, lsem):
    n_pass = p_ref.shape[0]
    dp = lax.axis_index("dp")
    tile = lax.axis_index("tile")
    x, z = lax.div(dp, NZ), lax.rem(dp, NZ)
    y, core = lax.div(tile, NC), lax.rem(tile, NC)

    def at(dx=0, dz=0, dy=0, dc=0):
        return (lax.rem(x + dx, NX) * NZ + lax.rem(z + dz, NZ),
                lax.rem(y + dy, NY) * NC + lax.rem(core + dc, NC))

    started = []

    def send(src, dst, where):
        i = len(started)
        copy = pltpu.make_async_remote_copy(
            src_ref=src, dst_ref=dst, send_sem=ssem.at[i], recv_sem=rsem.at[i],
            device_id=where, device_id_type=pl.DeviceIdType.MESH)
        copy.start()
        started.append(copy)
        return copy

    load_p = pltpu.make_async_copy(p_hbm, p_ref, lsem.at[0])
    load_p.start()

    barrier = pltpu.get_barrier_semaphore()
    partners = ([at(dx=d) for d in range(1, NX)] + [at(dz=d) for d in range(1, NZ)]
                + [at(dy=dy, dc=dc) for dy, dc in PLACE[1:]])
    for where in partners:
        pl.semaphore_signal(barrier, inc=1, device_id=where, device_id_type=pl.DeviceIdType.MESH)

    nq = q_ref.shape[0]
    cluster = qc_ref[...]
    owner = lax.shift_right_logical(cluster, 2)
    local = lax.bitwise_and(cluster, 3)
    n_owner = NX * NZ
    own = jnp.where(iota((n_owner, nq), 0) == owner, 1.0, 0.0)
    before = onehot(iota((nq, nq), 0) < iota((nq, nq), 1))
    rank = jnp.sum(own * nn(own.astype(BF16), before), axis=0, keepdims=True)
    first = jnp.sum(jnp.where(owner < iota((n_owner, nq), 0), 1.0, 0.0), axis=1, keepdims=True)
    order = (rank + jnp.sum(own * first, axis=0, keepdims=True)).astype(I32)
    rank = rank.astype(I32)
    carrier = lax.bitwise_and(order, 7)
    line = lax.shift_right_logical(order, 3)
    dxs = lax.bitwise_and(lax.shift_right_logical(owner, 3) - x, NX - 1)
    dzs = lax.bitwise_and(lax.bitwise_and(owner, NZ - 1) - z, NZ - 1)
    code = dxs * 32 + dzs * 4 + lax.shift_right_logical(rank, 3)
    mine = carrier == tile
    pick = onehot(iota((BLOCK, nq), 0) == jnp.where(mine, code, -1))
    row = iota((META, nq), 0)
    target = lax.bitwise_and(pos_ref[...], 8 * n_pass - 1)
    high = lax.shift_right_logical(target, 6)
    low = lax.bitwise_and(target, 63)
    digits = jnp.where(row == 69, high, jnp.where(row == 70, low, 0))
    digits = jnp.where((row == local + 64) | (row == 68), 1, digits)
    meta = nt(pick, digits.astype(F32).astype(BF16))
    meta = jnp.where(iota((BLOCK, META), 1) == 68, 1.0 - meta, meta)
    xs[:, :WIDTH] = nn(pick, q_ref[...]).astype(BF16)
    xs[:, WIDTH:] = meta.astype(BF16)

    pl.semaphore_wait(barrier, len(partners))

    x_copies = [send(xs.at[pl.ds(d * 32, 32)], xr.at[pl.ds(d * 32, 32)], at(dx=d)) for d in range(1, NX)]
    xr[pl.ds(0, 32)] = xs[pl.ds(0, 32)]

    clusters = pc_ref[...]
    lane_row = iota((META, n_pass), 0)
    off = jnp.where((lane_row == clusters - CL_OWN * dp + 64) | (lane_row > 68) | (lane_row < 64), 0.0, NEGATIVE)
    eye = onehot(iota((BLOCK, BLOCK), 0) == iota((BLOCK, BLOCK), 1))
    load_p.wait()
    lane = iota((n_pass, 128), 1)
    head = p_ref[:, :128].astype(F32)
    p0_ref[...] = jnp.where(lane < 64, head, off.T).astype(BF16)
    p1_ref[...] = jnp.where(lane < 64, 0.0, head).astype(BF16)

    i, c = iota((BLOCK, BLOCK), 0), iota((BLOCK, BLOCK), 1)
    to_z = onehot(c == lax.bitwise_and(lax.shift_right_logical(i, 2), 3) * 32
                  + lax.shift_right_logical(i, 4) * 4 + lax.bitwise_and(i, 3))
    to_x = onehot(c == lax.bitwise_and(lax.shift_right_logical(i, 2), 7) * 16
                  + lax.shift_right_logical(i, 5) * 4 + lax.bitwise_and(i, 3))
    for copy in x_copies:
        copy.wait_recv()
    zs[...] = nn(to_z, xr[...]).astype(BF16)
    z_copies = [send(zs.at[pl.ds(d * 16, 16)], agb.at[pl.ds(d * 16, 16)], at(dz=d)) for d in range(1, NZ)]
    agb[pl.ds(0, 16)] = zs[pl.ds(0, 16)]

    for b in range(WIDTH // 128):
        pt_ref[pl.ds(b * 128, 128)] = nt(eye, p_ref[:, b * 128:(b + 1) * 128]).astype(BF16)
    lines = nq // 8
    pick_line = onehot(iota((lines, nq), 0) == jnp.where(mine, line, -1))
    bsel_ref[...] = nt(pick_line, pick).astype(BF16)
    cdy = lax.bitwise_and(lax.shift_right_logical(carrier, 1) - y, NY - 1)
    cdc = lax.bitwise_and(carrier - core, 1)
    place = jnp.where(cdy == 0, cdc, jnp.where(cdy == 2, 6 + cdc, jnp.where(cdy == 1, 2, 3) + 2 * cdc))
    spread = onehot(iota((nq, nq), 0) == place * lines + line)
    fsel_ref[...] = nt(onehot(iota((nq, nq), 0) == iota((nq, nq), 1)), spread).astype(BF16)
    stat[...] = jnp.zeros_like(stat)
    lse_ref[...] = jnp.zeros_like(lse_ref)
    for copy in z_copies:
        copy.wait_recv()

    def gather_start(buf, rows):
        blk = lambda s: buf.at[pl.ds(s * rows, rows)]
        return [send(blk(0), blk(1), at(dc=1)), send(blk(0), blk(3), at(dy=1)), send(blk(0), blk(2), at(dy=3))]

    def gather_near(buf, rows, near):
        blk = lambda s: buf.at[pl.ds(s * rows, rows)]
        part = lambda s, h: buf.at[pl.ds(s * rows + h * (rows // 2), rows // 2)]
        near[1].wait_recv()
        near[2].wait_recv()
        return [send(part(3, 0), part(6, 0), at(dy=1)), send(part(2, 1), part(6, 1), at(dy=3)),
                send(blk(2), blk(4), at(dc=1)), send(blk(3), blk(5), at(dc=1))]

    def gather_far(buf, rows, far):
        blk = lambda s: buf.at[pl.ds(s * rows, rows)]
        far[0].wait_recv()
        far[1].wait_recv()
        return send(blk(6), blk(7), at(dc=1))

    stat_copies = [None] * 8

    def first_pass(pair):
        rows = pl.ds(pair * PAIR, PAIR)
        cols = pl.ds(pair * PAIR, PAIR)
        q0_ref[...] = jnp.where(iota((PAIR, 128), 1) < 64, agb[rows, 0:128].astype(F32),
                                agb[rows, WIDTH:ROW].astype(F32)).astype(BF16)
        step = 256

        def scores(j, tops):
            js = pl.ds(pl.multiple_of(j * step, step), step)
            value = nt(p0_ref[js], q0_ref[...])
            prob[0, js, cols] = value
            out = [jnp.maximum(tops[0], fold(value, jnp.max))]
            for m in range(1, 5):
                left = p1_ref[js] if m == 1 else p_ref[js, CUTS[m - 1]:CUTS[m]]
                right = agb[rows, 0:128] if m == 1 else agb[rows, CUTS[m - 1]:CUTS[m]]
                value = value + nt(left, right)
                prob[m, js, cols] = value
                out.append(jnp.maximum(tops[m], fold(value, jnp.max)))
            return tuple(out)

        tops = lax.fori_loop(0, n_pass // step, scores, (jnp.full((8, PAIR), -3e38, F32),) * 5)
        tops = [jnp.max(t, axis=0, keepdims=True) for t in tops]
        small = 64

        def exps(j, sums):
            js = pl.ds(pl.multiple_of(j * small, small), small)
            out = []
            for m in range(5):
                e = jnp.exp2((prob[m, js, cols] - tops[m]) * (SCALES[m] * LOG2E))
                prob[m, js, cols] = e
                out.append(sums[m] + fold(e, jnp.sum))
            return tuple(out)

        sums = lax.fori_loop(0, n_pass // small, exps, (jnp.zeros((8, PAIR), F32),) * 5)
        for m in range(5):
            top = tops[m] * SCALES[m]
            total = jnp.sum(sums[m], axis=0, keepdims=True)
            msc[m:m + 1, cols] = top
            lse = top + jnp.log(total)
            stat[2 * pair, m:m + 1] = lse[:, :BLOCK]
            stat[2 * pair + 1, m:m + 1] = lse[:, BLOCK:]
        for s in (2 * pair, 2 * pair + 1):
            if s:
                dy, dc = PLACE[s]
                stat_copies[s] = send(stat.at[s], stat_in.at[MIRROR[s]], at(dy=dy, dc=dc))

    near = gather_start(agb, BLOCK)
    near[0].wait_recv()
    first_pass(0)
    far = gather_near(agb, BLOCK, near)
    first_pass(1)
    last = gather_far(agb, BLOCK, far)
    far[2].wait_recv()
    far[3].wait_recv()
    first_pass(2)
    last.wait_recv()
    first_pass(3)

    for s in range(1, 8):
        stat_copies[s].wait_recv()
    parts = [stat[0]] + [stat_in[s] for s in range(1, 8)]
    top = functools.reduce(jnp.maximum, parts)
    lse_ref[0] = top + jnp.log(functools.reduce(jnp.add, [jnp.exp(v - top) for v in parts]))
    lse_copies = [None] * 8
    for s in range(7, 0, -1):
        dy, dc = PLACE[s]
        lse_copies[s] = send(lse_ref.at[0], lse_ref.at[MIRROR[s]], at(dy=dy, dc=dc))
    lse_from = {MIRROR[s]: lse_copies[s] for s in range(1, 8)}

    base = tile * n_pass
    pick_digit = jnp.where(iota((8, META), 1) == 69, 64.0,
                           jnp.where(iota((8, META), 1) == 70, 1.0, 0.0)).astype(BF16)

    def second_pass(pair):
        rows = pl.ds(pair * PAIR, PAIR)
        cols = pl.ds(pair * PAIR, PAIR)
        for s in (2 * pair, 2 * pair + 1):
            if s:
                lse_from[s].wait_recv()
        goal = nt(pick_digit, agb[rows, WIDTH:ROW])[0:1].astype(I32) - base
        lse = jnp.concatenate([lse_ref[2 * pair], lse_ref[2 * pair + 1]], axis=1)
        factor = [jnp.exp(msc[m:m + 1, cols] - lse[m:m + 1]) * SCALES[m] for m in range(5)]
        small = 64

        def weigh(j, carry):
            start = pl.multiple_of(j * small, small)
            js = pl.ds(start, small)
            hit = iota((small, PAIR), 0) == goal - start
            running = None
            for m in range(4, -1, -1):
                term = prob[m, js, cols] * factor[m]
                running = term if running is None else running + term
                drop = sum(SCALES[m:])
                wt[m, js, cols] = jnp.where(hit, running - drop, running).astype(BF16)
            return carry

        lax.fori_loop(0, n_pass // small, weigh, 0)
        for m in range(5):
            lo = CUTS[m - 1] if m else 0
            value = nn(pt_ref[lo:CUTS[m]], wt[m, :, cols]).astype(BF16)
            gt[2 * pair, lo:CUTS[m]] = value[:, :BLOCK]
            gt[2 * pair + 1, lo:CUTS[m]] = value[:, BLOCK:]

    def plus(*values):
        return functools.reduce(jnp.add, [v.astype(F32) for v in values])

    part = (pl.ds(0, HALF), pl.ds(HALF, HALF))
    second_pass(3)
    sib_far = send(gt.at[7], sib.at[3], at(dc=1))
    second_pass(2)
    sib_up = send(gt.at[4], sib.at[1], at(dc=1))
    sib_down = send(gt.at[5], sib.at[2], at(dc=1))
    sib_far.wait_recv()
    comb[2] = plus(gt[6], sib[3]).astype(BF16)
    half_up = send(comb.at[2, part[0]], half_in.at[0], at(dy=1))
    half_down = send(comb.at[2, part[1]], half_in.at[1], at(dy=3))
    second_pass(1)
    sib_up.wait_recv()
    sib_down.wait_recv()
    comb[0, part[1]] = plus(gt[2, part[1]], sib[1, part[1]]).astype(BF16)
    up_b = send(comb.at[0, part[1]], from_m.at[part[1]], at(dy=1))
    comb[1, part[0]] = plus(gt[3, part[0]], sib[2, part[0]]).astype(BF16)
    down_a = send(comb.at[1, part[0]], from_p.at[part[0]], at(dy=3))
    second_pass(0)
    sib_own = send(gt.at[1], sib.at[0], at(dc=1))
    half_up.wait_recv()
    half_down.wait_recv()
    comb[0, part[0]] = plus(gt[2, part[0]], sib[1, part[0]], half_in[0]).astype(BF16)
    up_a = send(comb.at[0, part[0]], from_m.at[part[0]], at(dy=1))
    comb[1, part[1]] = plus(gt[3, part[1]], sib[2, part[1]], half_in[1]).astype(BF16)
    down_b = send(comb.at[1, part[1]], from_p.at[part[1]], at(dy=3))

    step = 256

    def passage_part(j, carry):
        js = pl.ds(pl.multiple_of(j * step, step), step)
        low = nn(wt[0, js], agb[:, 0:128])
        high = nn(wt[1, js], agb[:, 0:128])
        pg_ref[js, 0:128] = jnp.where(iota((step, 128), 1) < 64, low, high).astype(BF16)
        for m in range(2, 5):
            pg_ref[js, CUTS[m - 1]:CUTS[m]] = nn(wt[m, js], agb[:, CUTS[m - 1]:CUTS[m]]).astype(BF16)
        return carry

    lax.fori_loop(0, n_pass // step, passage_part, 0)
    store_p = pltpu.make_async_copy(pg_ref, pg_hbm, lsem.at[1])
    store_p.start()

    for copy in (sib_own, up_a, up_b, down_a, down_b):
        copy.wait_recv()
    mine_t = plus(gt[0], sib[0], from_m[...], from_p[...]).astype(BF16)

    zbs[...] = nt(eye, mine_t).astype(BF16)
    z_back = [send(zbs.at[pl.ds(d * 16, 16)], zb.at[pl.ds(d * 16, 16)], at(dz=NZ - d)) for d in range(1, NZ)]
    zb[pl.ds(0, 16)] = zbs[pl.ds(0, 16)]
    for copy in z_back:
        copy.wait_recv()
    xbs[...] = nn(to_x, zb[...]).astype(BF16)
    x_back = [send(xbs.at[pl.ds(d * 32, 32)], xb.at[pl.ds(d * 32, 32)], at(dx=NX - d)) for d in range(1, NX)]
    xb[pl.ds(0, 32)] = xbs[pl.ds(0, 32)]
    for copy in x_back:
        copy.wait_recv()
    fg[pl.ds(0, lines)] = nn(bsel_ref[...], xb[...]).astype(BF16)
    near = gather_start(fg, lines)
    far = gather_near(fg, lines, near)
    last = gather_far(fg, lines, far)
    for copy in (near[0], far[2], far[3], last):
        copy.wait_recv()
    qg_ref[...] = nn(fsel_ref[...], fg[...]).astype(BF16)

    store_p.wait()
    for copy in started:
        copy.wait_send()


def body(queries, passages, query_cluster, passage_cluster, positive):
    nq, width = queries.shape
    n_pass = passages.shape[0]
    vmem = pl.BlockSpec(memory_space=pltpu.VMEM)
    hbm = pl.BlockSpec(memory_space=pl.ANY)
    V = pltpu.VMEM
    return pl.pallas_call(
        kernel,
        out_shape=(jax.ShapeDtypeStruct((nq, width), BF16), jax.ShapeDtypeStruct((n_pass, width), BF16)),
        in_specs=[vmem, vmem, vmem, vmem, hbm],
        out_specs=(vmem, hbm),
        scratch_shapes=[
            V((n_pass, width), BF16), V((n_pass, 128), BF16), V((n_pass, 128), BF16), V((width, n_pass), BF16),
            V((BLOCK, ROW), BF16), V((BLOCK, ROW), BF16), V((BLOCK, ROW), BF16), V((SLOTS, ROW), BF16),
            V((PAIR, 128), BF16),
            V((5, n_pass, SLOTS), F32), V((5, n_pass, SLOTS), BF16), V((8, SLOTS), F32),
            V((8, 8, BLOCK), F32), V((8, 8, BLOCK), F32), V((8, 8, BLOCK), F32),
            V((8, width, BLOCK), BF16), V((4, width, BLOCK), BF16), V((3, width, BLOCK), BF16),
            V((2, HALF, BLOCK), BF16), V((width, BLOCK), BF16), V((width, BLOCK), BF16),
            V((BLOCK, width), BF16), V((BLOCK, width), BF16), V((BLOCK, width), BF16), V((BLOCK, width), BF16),
            V((nq, width), BF16), V((nq // 8, BLOCK), BF16), V((nq, nq), BF16), V((n_pass, width), BF16),
            pltpu.SemaphoreType.DMA((72,)), pltpu.SemaphoreType.DMA((72,)), pltpu.SemaphoreType.DMA((2,)),
        ],
        compiler_params=pltpu.CompilerParams(
            collective_id=0, has_side_effects=True, vmem_limit_bytes=58 * 1024 * 1024),
    )(query_cluster.reshape(1, nq), positive.reshape(1, nq), passage_cluster.reshape(1, n_pass), queries, passages)


def solution(mesh):
    in_specs = (P("dp", None), P(("dp", "tile"), None), P("dp"), P(("dp", "tile")), P("dp"))
    out_specs = (P("dp", None), P(("dp", "tile"), None))
    return jax.shard_map(body, mesh=mesh, in_specs=in_specs, out_specs=out_specs, check_vma=False)
```

time: 343 us -> 84.4 us (0.25)
  waiting for transfers between devices: 145 us -> 0 us
  Pallas kernels: 0 us -> 80.1 us
  blocking collectives: 47.2 us -> 0 us
  matrix products: 39.8 us -> 0 us
  local copies, waits for them, and re-layouts: 36.3 us -> 3.33 us
  starting transfers between devices: 30.9 us -> 0 us
  other arithmetic: 25.7 us -> 0 us
  between operations: 14.2 us -> 0.65 us
    pallas_call x0 -> x1, Pallas kernels: none -> 80.1 us  [body(): pl.pallas_call(kernel, out_shape=(jax.ShapeDtypeStruct((nq, width), BF16)...]
    all_to_all x4 -> x0, waiting for transfers between devices: 79.7 us -> none  [the longest x1 35.7 us: body(): lax.all_to_all(send_rows, 'dp', split_axis=0, concat_axis=0, tiled=True)]
    psum x1 -> x0, waiting for transfers between devices: 65.1 us -> none  [body(): summed = lax.psum(query_partial.astype(jnp.bfloat16), 'tile')]
    dot_general x40 -> x0, matrix products: 39.8 us -> none  [the longest x20 22.3 us: contract(): lax.dot_general(left, right, (((1,), (1,)), ((), ())), preferred_element_...]
    all_to_all x4 -> x0, starting transfers between devices: 30.6 us -> none  [the longest x1 11.9 us: body(): lax.all_to_all(send_clusters, 'dp', split_axis=0, concat_axis=0, tiled=True)]
    psum x1 -> x0, blocking collectives: 23.8 us -> none  [body(): lax.psum(local_totals * jnp.exp(local_highest - global_highest), 'tile')]
    pmax x1 -> x0, blocking collectives: 23.4 us -> none  [body(): global_highest = lax.pmax(local_highest, 'tile')]
    reduce_sum x3 -> x0, other arithmetic: 11.4 us -> none  [the longest x2 11.3 us: first_pass(): jnp.sum(jnp.where(member, jnp.exp(value - highest[:, None]), 0.0), axis=1)]
  transfers between devices with their start and end apart: 5 -> 0, of which waited for: 5 -> 0; matrix products, arithmetic and copies ran while one was open for 3% -> 0% of each run, Pallas kernels for 0% -> 0%
where the time goes in v1:
time: 84.4 us; the launch traced here: 84.1 us
  Pallas kernels  80.1 us (95%)
  local copies, waits for them, and re-layouts  3.33 us (4%)
    pallas_call x1, Pallas kernels, body(): pl.pallas_call(kernel, out_shape=(jax.ShapeDtypeStruct((nq, width), BF16)...  80.1 us
    unnamed x4, local copies, waits for them, and re-layouts  3.33 us

profile of v1, /device:TPU:1, one launch (start us, length us, event | category | flops | bytes accessed | tf_op | source)
XLA Modules:
  0.0 84.1 jit_solution(4278803868659546934)
XLA Ops:
  0.6 80.1 %shard_map.68 = (bf16[512,768]{1,0:T(8,128)(2,1)}, bf16[1024,768]{1,0:T(8,128)(2,1)}) custom-call(s32[1,512]{1,0:T(1,128)} %bitcast.4, s32[1,512]{1,0:T(1,128)} %bitcast.5, s32[1,1024]{1,0:T(1,128)} %bitcast.3, bf16[512,768]{1,0:T(8,128)(2,1)} %q_ref.1, bf16[1024,768]{1,0:T(8,128)(2,1)} %p_hbm.1), custom_call_target="tpu_custom_call" | custom-call | tf_op jit(solution)/shard_map/pallas_call | solution.py:359
  80.7 0.0 copy-start
  80.7 2.2 %copy.9 = bf16[512,768]{1,0:T(8,128)(2,1)} copy(bf16[512,768]{1,0:T(8,128)(2,1)} %get-tuple-element.4) | data formatting | bytes 1572864
  82.9 0.0 copy-done
  82.9 1.1 %copy.10 = bf16[1024,768]{1,0:T(8,128)(2,1)} copy(bf16[1024,768]{1,0:T(8,128)(2,1)S(1)} %copy-done) | data formatting | bytes 3145728
Async XLA Ops:
  80.7 2.2 %copy-start = (bf16[1024,768]{1,0:T(8,128)(2,1)S(1)}, bf16[1024,768]{1,0:T(8,128)(2,1)}, u32[]{:S(2)}) copy-start(bf16[1024,768]{1,0:T(8,128)(2,1)} %get-tuple-element.5) | copy-start | bytes 4718596

commit v2 on v1

v2 whole, which is shorter than its diff:
```python
import functools
import math

import jax
import jax.numpy as jnp
from jax import lax
from jax.experimental import pallas as pl
from jax.experimental.pallas import tpu as pltpu
from jax.sharding import PartitionSpec as P

F32 = jnp.float32
BF16 = jnp.bfloat16
I32 = jnp.int32

NX, NZ, NY, NC = 4, 8, 4, 2
CL_OWN = 4
CAP = 32
NEGATIVE = -1e30
CUTS = (64, 128, 256, 512, 768)
WIDTH = 768
META = 128
ROW = WIDTH + META
SCALES = tuple(2.0 / math.sqrt(k) for k in CUTS)
LOG2E = math.log2(math.e)
BLOCK = 64
PAIR = 4 * BLOCK
HALF = 8 * BLOCK
SLOTS = 2 * HALF
FAR = NX * NZ
CHUNK = 16
STACK = ROW // 128 * BLOCK

PLACE = ((0, 0), (0, 1), (1, 0), (3, 0), (1, 1), (3, 1), (2, 0), (2, 1))
MIRROR = tuple(PLACE.index(((NY - dy) % NY, dc)) for dy, dc in PLACE)
MESH = pl.DeviceIdType.MESH


def nn(a, b):
    return lax.dot_general(a, b, (((1,), (0,)), ((), ())), preferred_element_type=F32)


def nt(a, b):
    return lax.dot_general(a, b, (((1,), (1,)), ((), ())), preferred_element_type=F32)


def iota(shape, dim):
    return lax.broadcasted_iota(I32, shape, dim)


def onehot(mask):
    return jnp.where(mask, 1.0, 0.0).astype(BF16)


def fold(value, op):
    return op(value.reshape(value.shape[0] // 8, 8, value.shape[1]), axis=0)


def plus(*values):
    return functools.reduce(jnp.add, [v.astype(F32) for v in values])


def shift(a, n):
    return lax.shift_right_logical(a, n)


def kernel(qc_ref, pos_ref, pc_ref, q_ref, p_hbm, qg_ref, pg_hbm,
           p_ref, p0_ref, p1_ref, pt_ref, stack, out_buf, in_buf, back_out, back_in, pack_ref, unpack_ref,
           agb, q0_ref, prob, wt, msc, stat, stat_in, lse_ref, gt, grad, sib, comb, from_y,
           rows_ref, fg, bsel_ref, fsel_ref, pg_ref,
           ssem, rsem, fsem, gsem, lsem):
    n_pass = p_ref.shape[0]
    dp = lax.axis_index("dp")
    tile = lax.axis_index("tile")
    x, z = lax.div(dp, NZ), lax.rem(dp, NZ)
    y, core = lax.div(tile, NC), lax.rem(tile, NC)

    def at(dy=0, dc=0):
        return (dp, lax.rem(y + dy, NY) * NC + lax.rem(core + dc, NC))

    def ahead(i):
        return (lax.rem(x + lax.div(i, NZ), NX) * NZ + lax.rem(z + lax.rem(i, NZ), NZ), tile)

    def behind(i):
        return (lax.rem(x + NX - lax.div(i, NZ), NX) * NZ + lax.rem(z + NZ - lax.rem(i, NZ), NZ), tile)

    started = []

    def send(src, dst, where):
        i = len(started)
        copy = pltpu.make_async_remote_copy(
            src_ref=src, dst_ref=dst, send_sem=ssem.at[i], recv_sem=rsem.at[i],
            device_id=where, device_id_type=MESH)
        copy.start()
        started.append(copy)
        return copy

    def chunk(i, src, dst, lane, where):
        rows = pl.ds(pl.multiple_of(i * CHUNK, CHUNK), CHUNK)
        return pltpu.make_async_remote_copy(
            src_ref=src.at[rows], dst_ref=dst.at[rows], send_sem=fsem.at[lane, i], recv_sem=gsem.at[lane, i],
            device_id=where(i), device_id_type=MESH)

    exchanges = []

    def exchange(src, dst, where):
        args = (src, dst, len(exchanges), where)
        exchanges.append(args)

        def go(i, carry):
            chunk(i, *args).start()
            return carry

        lax.fori_loop(1, FAR, go, 0)
        dst[pl.ds(0, CHUNK)] = src[pl.ds(0, CHUNK)]

        def arrived():
            def wait(i, carry):
                chunk(i, *args).wait_recv()
                return carry

            lax.fori_loop(1, FAR, wait, 0)

        return arrived

    load_p = pltpu.make_async_copy(p_hbm, p_ref, lsem.at[0])
    load_p.start()

    barrier = pltpu.get_barrier_semaphore()

    def greet(i, carry):
        pl.semaphore_signal(barrier, inc=1, device_id=ahead(i), device_id_type=MESH)
        return carry

    lax.fori_loop(1, FAR, greet, 0)
    for dy, dc in PLACE[1:]:
        pl.semaphore_signal(barrier, inc=1, device_id=at(dy, dc), device_id_type=MESH)

    nq = q_ref.shape[0]
    cluster = qc_ref[...]
    owner = shift(cluster, 2)
    local = lax.bitwise_and(cluster, 3)
    own = jnp.where(iota((FAR, nq), 0) == owner, 1.0, 0.0)
    before = onehot(iota((nq, nq), 0) < iota((nq, nq), 1))
    rank = jnp.sum(own * nn(own.astype(BF16), before), axis=0, keepdims=True)
    first = jnp.sum(jnp.where(owner < iota((FAR, nq), 0), 1.0, 0.0), axis=1, keepdims=True)
    order = (rank + jnp.sum(own * first, axis=0, keepdims=True)).astype(I32)
    rank = rank.astype(I32)
    carrier = lax.bitwise_and(order, 7)
    line = shift(order, 3)
    dxs = lax.bitwise_and(shift(owner, 3) - x, NX - 1)
    dzs = lax.bitwise_and(lax.bitwise_and(owner, NZ - 1) - z, NZ - 1)
    code = shift(rank, 4) * BLOCK + (dxs * NZ + dzs) * 2 + lax.bitwise_and(shift(rank, 3), 1)
    mine = carrier == tile
    pick = onehot(iota((2 * BLOCK, nq), 0) == jnp.where(mine, code, -1))
    row = iota((META, nq), 0)
    target = lax.bitwise_and(pos_ref[...], 8 * n_pass - 1)
    digits = jnp.where(row == 69, shift(target, 6), jnp.where(row == 70, lax.bitwise_and(target, 63), 0))
    digits = jnp.where((row == local + 64) | (row == 68), 1, digits)
    meta = nt(pick, digits.astype(F32).astype(BF16))
    meta = jnp.where(iota((2 * BLOCK, META), 1) == 68, 1.0 - meta, meta).astype(BF16)
    sent = nn(pick, q_ref[...]).astype(BF16)
    r, c = iota((HALF, STACK), 0), iota((HALF, STACK), 1)
    pack_ref[...] = onehot((shift(lax.bitwise_and(r, CHUNK - 1), 1) == shift(c, 6))
                           & (lax.bitwise_and(c, BLOCK - 1) == shift(r, 4) * 2 + lax.bitwise_and(r, 1)))
    c, r = iota((STACK, HALF), 0), iota((STACK, HALF), 1)
    unpack_ref[...] = onehot((shift(lax.bitwise_and(r, CHUNK - 1), 1) == shift(c, 6))
                             & (lax.bitwise_and(c, BLOCK - 1) == shift(r, 4) * 2 + lax.bitwise_and(r, 1)))
    for h in range(2):
        for b in range(WIDTH // 128):
            stack[pl.ds(b * BLOCK, BLOCK)] = sent[h * BLOCK:(h + 1) * BLOCK, b * 128:(b + 1) * 128]
        stack[pl.ds(STACK - BLOCK, BLOCK)] = meta[h * BLOCK:(h + 1) * BLOCK]
        out_buf[h] = nn(pack_ref[...], stack[...]).astype(BF16)

    pl.semaphore_wait(barrier, FAR - 1 + 7)

    arrived = [exchange(out_buf.at[h], in_buf.at[h], ahead) for h in range(2)]

    clusters = pc_ref[...]
    lane_row = iota((META, n_pass), 0)
    off = jnp.where((lane_row == clusters - CL_OWN * dp + 64) | (lane_row > 68) | (lane_row < 64), 0.0, NEGATIVE)
    load_p.wait()
    lane = iota((n_pass, 128), 1)
    head = p_ref[:, :128].astype(F32)
    p0_ref[...] = jnp.where(lane < 64, head, off.T).astype(BF16)
    p1_ref[...] = jnp.where(lane < 64, 0.0, head).astype(BF16)
    eye = onehot(iota((PAIR, PAIR), 0) == iota((PAIR, PAIR), 1))
    for b in range(WIDTH // PAIR):
        pt_ref[pl.ds(b * PAIR, PAIR)] = nt(eye, p_ref[:, b * PAIR:(b + 1) * PAIR]).astype(BF16)
    lines = nq // 8
    pick_line = onehot(iota((lines, nq), 0) == jnp.where(mine, line, -1))
    bsel_ref[...] = nt(pick_line, pick).astype(BF16)
    cdy = lax.bitwise_and(shift(carrier, 1) - y, NY - 1)
    cdc = lax.bitwise_and(carrier - core, 1)
    place = jnp.where(cdy == 0, cdc, jnp.where(cdy == 2, 6 + cdc, jnp.where(cdy == 1, 2, 3) + 2 * cdc))
    spread = onehot(iota((nq, nq), 0) == place * lines + line)
    fsel_ref[...] = nt(onehot(iota((nq, nq), 0) == iota((nq, nq), 1)), spread).astype(BF16)
    stat[...] = jnp.zeros_like(stat)
    lse_ref[...] = jnp.zeros_like(lse_ref)

    def gather_start(buf, base, rows):
        blk = lambda s: buf.at[pl.ds(base + s * rows, rows)]
        return {1: send(blk(0), blk(1), at(dc=1)), 3: send(blk(0), blk(3), at(dy=1)),
                2: send(blk(0), blk(2), at(dy=3)), 6: send(blk(0), blk(6), at(dy=2))}

    def gather_pass(buf, base, rows, got, s):
        blk = lambda s: buf.at[pl.ds(base + s * rows, rows)]
        got[s].wait_recv()
        on = {2: 4, 3: 5, 6: 7}[s]
        got[on] = send(blk(s), blk(on), at(dc=1))

    got = []
    for h in range(2):
        arrived[h]()
        rows = nn(unpack_ref[...], in_buf[h]).astype(BF16)
        for b in range(ROW // 128):
            agb[pl.ds(h * HALF, BLOCK), b * 128:(b + 1) * 128] = rows[b * BLOCK:(b + 1) * BLOCK]
        got.append(gather_start(agb, h * HALF, BLOCK))

    stat_copies = {}

    def first_pass(u):
        h, q = u // 2, u % 2
        rows = pl.ds(u * PAIR, PAIR)
        cols = pl.ds(u * PAIR, PAIR)
        q0_ref[...] = jnp.where(iota((PAIR, 128), 1) < 64, agb[rows, 0:128].astype(F32),
                                agb[rows, WIDTH:ROW].astype(F32)).astype(BF16)
        value, tops = None, []
        for m in range(5):
            left = (p0_ref[...], p1_ref[...])[m] if m < 2 else p_ref[:, CUTS[m - 1]:CUTS[m]]
            right = (q0_ref[...], agb[rows, 0:128])[m] if m < 2 else agb[rows, CUTS[m - 1]:CUTS[m]]
            part = nt(left, right)
            value = part if value is None else value + part
            prob[m, :, cols] = value
            tops.append(jnp.max(fold(value, jnp.max), axis=0, keepdims=True))
        small = 128

        def exps(j, sums):
            js = pl.ds(pl.multiple_of(j * small, small), small)
            out = []
            for m in range(5):
                e = jnp.exp2((prob[m, js, cols] - tops[m]) * (SCALES[m] * LOG2E))
                prob[m, js, cols] = e
                out.append(sums[m] + fold(e, jnp.sum))
            return tuple(out)

        sums = lax.fori_loop(0, n_pass // small, exps, (jnp.zeros((8, PAIR), F32),) * 5)
        for m in range(5):
            top = tops[m] * SCALES[m]
            total = jnp.sum(sums[m], axis=0, keepdims=True)
            msc[m:m + 1, cols] = top
            lse = top + jnp.log(total)
            for s in range(4):
                stat[h, 4 * q + s, m:m + 1] = lse[:, s // 2 * 128:s // 2 * 128 + 128]
        for s in range(4 * q, 4 * q + 4):
            if s:
                stat_copies[h, s] = send(stat.at[h, s], stat_in.at[h, MIRROR[s]], at(*PLACE[s]))

    lse_from = {}

    def totals(h):
        parts = [stat[h, 0]]
        for s in range(1, 8):
            stat_copies[h, s].wait_recv()
        for s in range(1, 8):
            value = stat_in[h, MIRROR[s]]
            parts.append(pltpu.roll(value, BLOCK, 1) if s % 2 else value)
        top = functools.reduce(jnp.maximum, parts)
        lse = top + jnp.log(functools.reduce(jnp.add, [jnp.exp(v - top) for v in parts]))
        lse_ref[h, 0] = jnp.where(iota((8, 128), 1) < BLOCK, lse, pltpu.roll(lse, BLOCK, 1))
        for s in range(7, 0, -1):
            lse_from[h, MIRROR[s]] = send(lse_ref.at[h, 0], lse_ref.at[h, MIRROR[s]], at(*PLACE[s]))

    base = tile * n_pass
    pick_digit = jnp.where(iota((8, META), 1) == 69, 64.0,
                           jnp.where(iota((8, META), 1) == 70, 1.0, 0.0)).astype(BF16)

    def second_pass(u, between=None):
        h, q = u // 2, u % 2
        rows = pl.ds(u * PAIR, PAIR)
        cols = pl.ds(u * PAIR, PAIR)
        for s in range(4 * q, 4 * q + 4):
            if s:
                lse_from[h, s].wait_recv()
        goal = nt(pick_digit, agb[rows, WIDTH:ROW])[0:1].astype(I32) - base
        lower = iota((8, 128), 1) < BLOCK
        lse = jnp.concatenate([jnp.where(lower, lse_ref[h, 4 * q + s], lse_ref[h, 4 * q + s + 1]) for s in (0, 2)],
                              axis=1)
        factor = [jnp.exp(msc[m:m + 1, cols] - lse[m:m + 1]) * SCALES[m] for m in range(5)]
        small = 64

        def weigh(j, carry):
            start = pl.multiple_of(j * small, small)
            js = pl.ds(start, small)
            hit = iota((small, PAIR), 0) == goal - start
            running = None
            for m in range(4, -1, -1):
                term = prob[m, js, cols] * factor[m]
                running = term if running is None else running + term
                wt[m, js, cols] = jnp.where(hit, running - sum(SCALES[m:]), running).astype(BF16)
            return carry

        lax.fori_loop(0, n_pass // small, weigh, 0)
        if between is not None:
            between()
        for m in range(5):
            lo = CUTS[m - 1] if m else 0
            gt[lo:CUTS[m]] = nn(pt_ref[lo:CUTS[m]], wt[m, :, cols]).astype(BF16)
        grad[rows] = nt(eye, gt[...]).astype(BF16)

    sums_in = {}

    def block(h, s):
        return grad.at[pl.ds(h * HALF + s * BLOCK, BLOCK)]

    def to_core(h, s):
        i = {1: 0, 4: 1, 5: 2, 7: 3}[s]
        sums_in[h, i] = send(block(h, s), sib.at[h, i], at(dc=1))

    def to_chip(h, s):
        i = {2: 1, 3: 2, 6: 3}[s]
        sums_in[h, i].wait_recv()
        comb[h, i] = plus(block(h, s)[...], sib[h, i]).astype(BF16)
        sums_in[h, s, s] = send(comb.at[h, i], from_y.at[h, i], at(dy=PLACE[s][0]))

    def go_back(h):
        sums_in[h, 0].wait_recv()
        for s in (2, 3, 6):
            sums_in[h, s, s].wait_recv()
        total = plus(block(h, 0)[...], sib[h, 0], from_y[h, 1], from_y[h, 2], from_y[h, 3]).astype(BF16)
        for b in range(WIDTH // 128):
            stack[pl.ds(b * BLOCK, BLOCK)] = total[:, b * 128:(b + 1) * 128]
        used = WIDTH // 128 * BLOCK
        back_out[h] = nn(pack_ref[:, :used], stack[pl.ds(0, used)]).astype(BF16)
        return exchange(back_out.at[h], back_in.at[h], behind)

    wide = n_pass // 2

    def passage_part(j):
        js = slice(j * wide, (j + 1) * wide)
        low = nn(wt[0, js], agb[:, 0:128])
        high = nn(wt[1, js], agb[:, 0:128])
        pg_ref[js, 0:128] = jnp.where(iota((wide, 128), 1) < 64, low, high).astype(BF16)
        for m in range(2, 5):
            pg_ref[js, CUTS[m - 1]:CUTS[m]] = nn(wt[m, js], agb[:, CUTS[m - 1]:CUTS[m]]).astype(BF16)
        store = pltpu.make_async_copy(pg_ref.at[js], pg_hbm.at[js], lsem.at[1 + j])
        store.start()
        return store

    def gather_near(h):
        gather_pass(agb, h * HALF, BLOCK, got[h], 2)
        gather_pass(agb, h * HALF, BLOCK, got[h], 3)
        got[h][1].wait_recv()

    def gather_rest(h):
        gather_pass(agb, h * HALF, BLOCK, got[h], 6)
        for s in (4, 5, 7):
            got[h][s].wait_recv()

    gather_near(0)
    first_pass(0)
    gather_rest(0)
    first_pass(1)
    gather_near(1)
    first_pass(2)
    totals(0)
    gather_rest(1)
    first_pass(3)

    second_pass(1)
    for s in (7, 4, 5):
        to_core(0, s)
    totals(1)
    second_pass(0, lambda: to_chip(0, 6))
    to_core(0, 1)
    to_chip(0, 2)
    to_chip(0, 3)
    second_pass(3)
    for s in (7, 4, 5):
        to_core(1, s)
    second_pass(2, lambda: to_chip(1, 6))
    to_core(1, 1)
    to_chip(1, 2)
    to_chip(1, 3)
    home = [go_back(0)]
    stores = [passage_part(0)]
    home.append(go_back(1))
    stores.append(passage_part(1))

    for h in range(2):
        home[h]()
        used = WIDTH // 128 * BLOCK
        rows = nn(unpack_ref[:used], back_in[h]).astype(BF16)
        for b in range(WIDTH // 128):
            rows_ref[pl.ds(h * BLOCK, BLOCK), b * 128:(b + 1) * 128] = rows[b * BLOCK:(b + 1) * BLOCK]
    fg[pl.ds(0, lines)] = nn(bsel_ref[...], rows_ref[...]).astype(BF16)
    last = gather_start(fg, 0, lines)
    for s in (2, 3, 6):
        gather_pass(fg, 0, lines, last, s)
    for s in (1, 4, 5, 7):
        last[s].wait_recv()
    qg_ref[...] = nn(fsel_ref[...], fg[...]).astype(BF16)

    for store in stores:
        store.wait()
    for copy in started:
        copy.wait_send()
    for args in exchanges:
        def sent_all(i, carry, args=args):
            chunk(i, *args).wait_send()
            return carry

        lax.fori_loop(1, FAR, sent_all, 0)


def body(queries, passages, query_cluster, passage_cluster, positive):
    nq, width = queries.shape
    n_pass = passages.shape[0]
    vmem = pl.BlockSpec(memory_space=pltpu.VMEM)
    hbm = pl.BlockSpec(memory_space=pl.ANY)
    V = pltpu.VMEM
    return pl.pallas_call(
        kernel,
        out_shape=(jax.ShapeDtypeStruct((nq, width), BF16), jax.ShapeDtypeStruct((n_pass, width), BF16)),
        in_specs=[vmem, vmem, vmem, vmem, hbm],
        out_specs=(vmem, hbm),
        scratch_shapes=[
            V((n_pass, width), BF16), V((n_pass, 128), BF16), V((n_pass, 128), BF16), V((width, n_pass), BF16),
            V((STACK, 128), BF16), *[V((2, HALF, 128), BF16)] * 4, V((HALF, STACK), BF16), V((STACK, HALF), BF16),
            V((SLOTS, ROW), BF16), V((PAIR, 128), BF16),
            V((5, n_pass, SLOTS), F32), V((5, n_pass, SLOTS), BF16), V((8, SLOTS), F32),
            V((2, 8, 8, 128), F32), V((2, 8, 8, 128), F32), V((2, 8, 8, 128), F32),
            V((width, PAIR), BF16), V((SLOTS, width), BF16),
            V((2, 4, BLOCK, width), BF16), V((2, 4, BLOCK, width), BF16), V((2, 4, BLOCK, width), BF16),
            V((2 * BLOCK, width), BF16), V((nq, width), BF16), V((nq // 8, 2 * BLOCK), BF16), V((nq, nq), BF16),
            V((n_pass, width), BF16),
            pltpu.SemaphoreType.DMA((72,)), pltpu.SemaphoreType.DMA((72,)),
            pltpu.SemaphoreType.DMA((4, FAR)), pltpu.SemaphoreType.DMA((4, FAR)), pltpu.SemaphoreType.DMA((3,)),
        ],
        compiler_params=pltpu.CompilerParams(
            collective_id=0, has_side_effects=True, vmem_limit_bytes=58 * 1024 * 1024),
    )(query_cluster.reshape(1, nq), positive.reshape(1, nq), passage_cluster.reshape(1, n_pass), queries, passages)


def solution(mesh):
    in_specs = (P("dp", None), P(("dp", "tile"), None), P("dp"), P(("dp", "tile")), P("dp"))
    out_specs = (P("dp", None), P(("dp", "tile"), None))
    return jax.shard_map(body, mesh=mesh, in_specs=in_specs, out_specs=out_specs, check_vma=False)
```

time: 84.4 us -> 81.4 us (0.964)
  Pallas kernels: 80.1 us -> 77.3 us
    pallas_call x1, Pallas kernels: 80.1 us -> 77.3 us  [body(): pl.pallas_call(kernel, out_shape=(jax.ShapeDtypeStruct((nq, width), BF16)...]
where the time goes in v2:
time: 81.4 us; the launch traced here: 81.3 us
  Pallas kernels  77.3 us (95%)
  local copies, waits for them, and re-layouts  3.33 us (4%)
    pallas_call x1, Pallas kernels, body(): pl.pallas_call(kernel, out_shape=(jax.ShapeDtypeStruct((nq, width), BF16)...  77.3 us
    unnamed x4, local copies, waits for them, and re-layouts  3.33 us

profile of v2, /device:TPU:1, one launch (start us, length us, event | category | flops | bytes accessed | tf_op | source)
XLA Modules:
  0.0 81.3 jit_solution(11392363473395063552)
XLA Ops:
  0.6 77.3 %shard_map.68 = (bf16[512,768]{1,0:T(8,128)(2,1)}, bf16[1024,768]{1,0:T(8,128)(2,1)}) custom-call(s32[1,512]{1,0:T(1,128)} %bitcast.4, s32[1,512]{1,0:T(1,128)} %bitcast.5, s32[1,1024]{1,0:T(1,128)} %bitcast.3, bf16[512,768]{1,0:T(8,128)(2,1)} %q_ref.1, bf16[1024,768]{1,0:T(8,128)(2,1)} %p_hbm.1), custom_call_target="tpu_custom_call" | custom-call | tf_op jit(solution)/shard_map/pallas_call | solution.py:421
  78.0 0.0 copy-start
  78.0 2.2 %copy.9 = bf16[512,768]{1,0:T(8,128)(2,1)} copy(bf16[512,768]{1,0:T(8,128)(2,1)} %get-tuple-element.4) | data formatting | bytes 1572864
  80.2 0.0 copy-done
  80.2 1.1 %copy.10 = bf16[1024,768]{1,0:T(8,128)(2,1)} copy(bf16[1024,768]{1,0:T(8,128)(2,1)S(1)} %copy-done) | data formatting | bytes 3145728
Async XLA Ops:
  78.0 2.2 %copy-start = (bf16[1024,768]{1,0:T(8,128)(2,1)S(1)}, bf16[1024,768]{1,0:T(8,128)(2,1)}, u32[]{:S(2)}) copy-start(bf16[1024,768]{1,0:T(8,128)(2,1)} %get-tuple-element.5) | copy-start | bytes 4718596

commit v3 on v2

--- a/solution.py
+++ b/solution.py
@@ -33,6 +33,7 @@
 PLACE = ((0, 0), (0, 1), (1, 0), (3, 0), (1, 1), (3, 1), (2, 0), (2, 1))
 MIRROR = tuple(PLACE.index(((NY - dy) % NY, dc)) for dy, dc in PLACE)
 MESH = pl.DeviceIdType.MESH
+PARTS = 4
 
 
 def nn(a, b):
@@ -63,11 +64,11 @@
     return lax.shift_right_logical(a, n)
 
 
-def kernel(qc_ref, pos_ref, pc_ref, q_ref, p_hbm, qg_ref, pg_hbm,
-           p_ref, p0_ref, p1_ref, pt_ref, stack, out_buf, in_buf, back_out, back_in, pack_ref, unpack_ref,
+def kernel(qc_ref, pos_ref, pc_ref, q_hbm, p_hbm, fg_hbm, fsel_hbm, pg_hbm,
+           q_ref, p_ref, p0_ref, p1_ref, pt_ref, stack, out_buf, in_buf, back_out, back_in, pack_ref, unpack_ref,
            agb, q0_ref, prob, wt, msc, stat, stat_in, lse_ref, gt, grad, sib, comb, from_y,
            rows_ref, fg, bsel_ref, fsel_ref, pg_ref,
-           ssem, rsem, fsem, gsem, lsem):
+           ssem, rsem, lsem):
     n_pass = p_ref.shape[0]
     dp = lax.axis_index("dp")
     tile = lax.axis_index("tile")
@@ -83,57 +84,48 @@
     def behind(i):
         return (lax.rem(x + NX - lax.div(i, NZ), NX) * NZ + lax.rem(z + NZ - lax.rem(i, NZ), NZ), tile)
 
-    started = []
-
-    def send(src, dst, where):
-        i = len(started)
-        copy = pltpu.make_async_remote_copy(
-            src_ref=src, dst_ref=dst, send_sem=ssem.at[i], recv_sem=rsem.at[i],
-            device_id=where, device_id_type=MESH)
+    groups, received = [], []
+
+    def group(all_sent):
+        groups.append(all_sent)
+        return len(groups) - 1
+
+    def arrival():
+        received.append(None)
+        return len(received) - 1
+
+    def remote(src, dst, g, i, where):
+        return pltpu.make_async_remote_copy(
+            src_ref=src, dst_ref=dst, send_sem=ssem.at[g], recv_sem=rsem.at[i], device_id=where, device_id_type=MESH)
+
+    def send(src, dst, where, g, i=None):
+        copy = remote(src, dst, g, arrival() if i is None else i, where)
         copy.start()
-        started.append(copy)
         return copy
 
-    def chunk(i, src, dst, lane, where):
-        rows = pl.ds(pl.multiple_of(i * CHUNK, CHUNK), CHUNK)
-        return pltpu.make_async_remote_copy(
-            src_ref=src.at[rows], dst_ref=dst.at[rows], send_sem=fsem.at[lane, i], recv_sem=gsem.at[lane, i],
-            device_id=where(i), device_id_type=MESH)
-
-    exchanges = []
-
     def exchange(src, dst, where):
-        args = (src, dst, len(exchanges), where)
-        exchanges.append(args)
+        rest = pl.ds(CHUNK, (FAR - 1) * CHUNK)
+        g, n = group(src.at[rest]), arrival()
 
         def go(i, carry):
-            chunk(i, *args).start()
+            rows = pl.ds(pl.multiple_of(i * CHUNK, CHUNK), CHUNK)
+            remote(src.at[rows], dst.at[rows], g, n, where(i)).start()
             return carry
 
         lax.fori_loop(1, FAR, go, 0)
         dst[pl.ds(0, CHUNK)] = src[pl.ds(0, CHUNK)]
-
-        def arrived():
-            def wait(i, carry):
-                chunk(i, *args).wait_recv()
-                return carry
-
-            lax.fori_loop(1, FAR, wait, 0)
-
-        return arrived
-
+        return remote(src.at[rest], dst.at[rest], g, n, where(1)).wait_recv
+
+    barrier = pltpu.get_barrier_semaphore()
+    for dx, dz in sorted(((i // NZ, i % NZ) for i in range(1, FAR)), key=lambda d: abs(d[1] - NZ // 2)):
+        there = lax.rem(x + dx, NX) * NZ + lax.rem(z + dz, NZ)
+        pl.semaphore_signal(barrier, inc=1, device_id=(there, tile), device_id_type=MESH)
+    for dy, dc in PLACE[1:]:
+        pl.semaphore_signal(barrier, inc=1, device_id=at(dy, dc), device_id_type=MESH)
+    load_q = pltpu.make_async_copy(q_hbm, q_ref, lsem.at[3])
+    load_q.start()
     load_p = pltpu.make_async_copy(p_hbm, p_ref, lsem.at[0])
     load_p.start()
-
-    barrier = pltpu.get_barrier_semaphore()
-
-    def greet(i, carry):
-        pl.semaphore_signal(barrier, inc=1, device_id=ahead(i), device_id_type=MESH)
-        return carry
-
-    lax.fori_loop(1, FAR, greet, 0)
-    for dy, dc in PLACE[1:]:
-        pl.semaphore_signal(barrier, inc=1, device_id=at(dy, dc), device_id_type=MESH)
 
     nq = q_ref.shape[0]
     cluster = qc_ref[...]
@@ -158,6 +150,7 @@
     digits = jnp.where((row == local + 64) | (row == 68), 1, digits)
     meta = nt(pick, digits.astype(F32).astype(BF16))
     meta = jnp.where(iota((2 * BLOCK, META), 1) == 68, 1.0 - meta, meta).astype(BF16)
+    load_q.wait()
     sent = nn(pick, q_ref[...]).astype(BF16)
     r, c = iota((HALF, STACK), 0), iota((HALF, STACK), 1)
     pack_ref[...] = onehot((shift(lax.bitwise_and(r, CHUNK - 1), 1) == shift(c, 6))
@@ -194,19 +187,22 @@
     place = jnp.where(cdy == 0, cdc, jnp.where(cdy == 2, 6 + cdc, jnp.where(cdy == 1, 2, 3) + 2 * cdc))
     spread = onehot(iota((nq, nq), 0) == place * lines + line)
     fsel_ref[...] = nt(onehot(iota((nq, nq), 0) == iota((nq, nq), 1)), spread).astype(BF16)
+    stores = [pltpu.make_async_copy(fsel_ref, fsel_hbm, lsem.at[4])]
+    stores[0].start()
     stat[...] = jnp.zeros_like(stat)
     lse_ref[...] = jnp.zeros_like(lse_ref)
 
     def gather_start(buf, base, rows):
         blk = lambda s: buf.at[pl.ds(base + s * rows, rows)]
-        return {1: send(blk(0), blk(1), at(dc=1)), 3: send(blk(0), blk(3), at(dy=1)),
-                2: send(blk(0), blk(2), at(dy=3)), 6: send(blk(0), blk(6), at(dy=2))}
+        g = group(buf.at[pl.ds(base, 7 * rows)])
+        return {0: g, 1: send(blk(0), blk(1), at(dc=1), g), 3: send(blk(0), blk(3), at(dy=1), g),
+                2: send(blk(0), blk(2), at(dy=3), g), 6: send(blk(0), blk(6), at(dy=2), g)}
 
     def gather_pass(buf, base, rows, got, s):
         blk = lambda s: buf.at[pl.ds(base + s * rows, rows)]
         got[s].wait_recv()
         on = {2: 4, 3: 5, 6: 7}[s]
-        got[on] = send(blk(s), blk(on), at(dc=1))
+        got[on] = send(blk(s), blk(on), at(dc=1), got[0])
 
     got = []
     for h in range(2):
@@ -216,7 +212,11 @@
             agb[pl.ds(h * HALF, BLOCK), b * 128:(b + 1) * 128] = rows[b * BLOCK:(b + 1) * BLOCK]
         got.append(gather_start(agb, h * HALF, BLOCK))
 
-    stat_copies = {}
+    others = pl.ds(1, 7)
+    stat_group = [group(stat.at[h, others]) for h in range(2)]
+    stat_come = [arrival() for h in range(2)]
+    lse_group = [group(lse_ref.at[h, others]) for h in range(2)]
+    lse_come = [arrival() for h in range(2)]
 
     def first_pass(u):
         h, q = u // 2, u % 2
@@ -253,14 +253,11 @@
                 stat[h, 4 * q + s, m:m + 1] = lse[:, s // 2 * 128:s // 2 * 128 + 128]
         for s in range(4 * q, 4 * q + 4):
             if s:
-                stat_copies[h, s] = send(stat.at[h, s], stat_in.at[h, MIRROR[s]], at(*PLACE[s]))
-
-    lse_from = {}
+                send(stat.at[h, s], stat_in.at[h, MIRROR[s]], at(*PLACE[s]), stat_group[h], stat_come[h])
 
     def totals(h):
         parts = [stat[h, 0]]
-        for s in range(1, 8):
-            stat_copies[h, s].wait_recv()
+        remote(stat.at[h, others], stat_in.at[h, others], stat_group[h], stat_come[h], at(dc=1)).wait_recv()
         for s in range(1, 8):
             value = stat_in[h, MIRROR[s]]
             parts.append(pltpu.roll(value, BLOCK, 1) if s % 2 else value)
@@ -268,7 +265,7 @@
         lse = top + jnp.log(functools.reduce(jnp.add, [jnp.exp(v - top) for v in parts]))
         lse_ref[h, 0] = jnp.where(iota((8, 128), 1) < BLOCK, lse, pltpu.roll(lse, BLOCK, 1))
         for s in range(7, 0, -1):
-            lse_from[h, MIRROR[s]] = send(lse_ref.at[h, 0], lse_ref.at[h, MIRROR[s]], at(*PLACE[s]))
+            send(lse_ref.at[h, 0], lse_ref.at[h, MIRROR[s]], at(*PLACE[s]), lse_group[h], lse_come[h])
 
     base = tile * n_pass
     pick_digit = jnp.where(iota((8, META), 1) == 69, 64.0,
@@ -278,9 +275,8 @@
         h, q = u // 2, u % 2
         rows = pl.ds(u * PAIR, PAIR)
         cols = pl.ds(u * PAIR, PAIR)
-        for s in range(4 * q, 4 * q + 4):
-            if s:
-                lse_from[h, s].wait_recv()
+        if q == 1:
+            remote(lse_ref.at[h, others], lse_ref.at[h, others], lse_group[h], lse_come[h], at(dc=1)).wait_recv()
         goal = nt(pick_digit, agb[rows, WIDTH:ROW])[0:1].astype(I32) - base
         lower = iota((8, 128), 1) < BLOCK
         lse = jnp.concatenate([jnp.where(lower, lse_ref[h, 4 * q + s], lse_ref[h, 4 * q + s + 1]) for s in (0, 2)],
@@ -308,19 +304,20 @@
         grad[rows] = nt(eye, gt[...]).astype(BF16)
 
     sums_in = {}
+    sum_group = [group(grad.at[pl.ds(h * HALF, 7 * BLOCK)]) for h in range(2)]
 
     def block(h, s):
         return grad.at[pl.ds(h * HALF + s * BLOCK, BLOCK)]
 
     def to_core(h, s):
         i = {1: 0, 4: 1, 5: 2, 7: 3}[s]
-        sums_in[h, i] = send(block(h, s), sib.at[h, i], at(dc=1))
+        sums_in[h, i] = send(block(h, s), sib.at[h, i], at(dc=1), sum_group[h])
 
     def to_chip(h, s):
         i = {2: 1, 3: 2, 6: 3}[s]
         sums_in[h, i].wait_recv()
         comb[h, i] = plus(block(h, s)[...], sib[h, i]).astype(BF16)
-        sums_in[h, s, s] = send(comb.at[h, i], from_y.at[h, i], at(dy=PLACE[s][0]))
+        sums_in[h, s, s] = send(comb.at[h, i], from_y.at[h, i], at(dy=PLACE[s][0]), sum_group[h])
 
     def go_back(h):
         sums_in[h, 0].wait_recv()
@@ -382,7 +379,7 @@
     to_chip(1, 2)
     to_chip(1, 3)
     home = [go_back(0)]
-    stores = [passage_part(0)]
+    stores.append(passage_part(0))
     home.append(go_back(1))
     stores.append(passage_part(1))
 
@@ -398,18 +395,40 @@
         gather_pass(fg, 0, lines, last, s)
     for s in (1, 4, 5, 7):
         last[s].wait_recv()
-    qg_ref[...] = nn(fsel_ref[...], fg[...]).astype(BF16)
-
+    assert len(groups) == ssem.shape[0] and len(received) == rsem.shape[0]
+    write = pltpu.make_async_copy(fg, fg_hbm, lsem.at[3])
+    write.start()
+    write.wait()
     for store in stores:
         store.wait()
-    for copy in started:
-        copy.wait_send()
-    for args in exchanges:
-        def sent_all(i, carry, args=args):
-            chunk(i, *args).wait_send()
-            return carry
-
-        lax.fori_loop(1, FAR, sent_all, 0)
+    for g, all_sent in enumerate(groups):
+        remote(all_sent, all_sent, g, 0, at(dc=1)).wait_send()
+
+
+def finish(fsel_hbm, fg_hbm, pg_hbm, qg_hbm, out_hbm, fsel_ref, fg_ref, qg_ref, pg_ref, sems):
+    loads = [pltpu.make_async_copy(fsel_hbm, fsel_ref, sems.at[0]), pltpu.make_async_copy(fg_hbm, fg_ref, sems.at[1])]
+    for load in loads:
+        load.start()
+    rows = pg_hbm.shape[0] // PARTS
+    parts = [pl.ds(i * rows, rows) for i in range(PARTS)]
+    reads = [pltpu.make_async_copy(pg_hbm.at[r], pg_ref.at[r], sems.at[2 + i]) for i, r in enumerate(parts)]
+    writes = [pltpu.make_async_copy(pg_ref.at[r], out_hbm.at[r], sems.at[2 + PARTS + i]) for i, r in enumerate(parts)]
+    for read in reads:
+        read.start()
+    for load in loads:
+        load.wait()
+    for read, write in zip(reads, writes):
+        read.wait()
+        write.start()
+    some = qg_ref.shape[0] // 2
+    for i in range(2):
+        r = pl.ds(i * some, some)
+        qg_ref[r] = nn(fsel_ref[r], fg_ref[...]).astype(BF16)
+        write = pltpu.make_async_copy(qg_ref.at[r], qg_hbm.at[r], sems.at[2 + 2 * PARTS + i])
+        write.start()
+        writes.append(write)
+    for write in writes:
+        write.wait()
 
 
 def body(queries, passages, query_cluster, passage_cluster, positive):
@@ -418,12 +437,14 @@
     vmem = pl.BlockSpec(memory_space=pltpu.VMEM)
     hbm = pl.BlockSpec(memory_space=pl.ANY)
     V = pltpu.VMEM
-    return pl.pallas_call(
+    fg, fsel, pg = pl.pallas_call(
         kernel,
-        out_shape=(jax.ShapeDtypeStruct((nq, width), BF16), jax.ShapeDtypeStruct((n_pass, width), BF16)),
-        in_specs=[vmem, vmem, vmem, vmem, hbm],
-        out_specs=(vmem, hbm),
+        out_shape=(jax.ShapeDtypeStruct((nq, width), BF16), jax.ShapeDtypeStruct((nq, nq), BF16),
+                   jax.ShapeDtypeStruct((n_pass, width), BF16)),
+        in_specs=[vmem, vmem, vmem, hbm, hbm],
+        out_specs=(hbm, hbm, hbm),
         scratch_shapes=[
+            V((nq, width), BF16),
             V((n_pass, width), BF16), V((n_pass, 128), BF16), V((n_pass, 128), BF16), V((width, n_pass), BF16),
             V((STACK, 128), BF16), *[V((2, HALF, 128), BF16)] * 4, V((HALF, STACK), BF16), V((STACK, HALF), BF16),
             V((SLOTS, ROW), BF16), V((PAIR, 128), BF16),
@@ -433,12 +454,20 @@
             V((2, 4, BLOCK, width), BF16), V((2, 4, BLOCK, width), BF16), V((2, 4, BLOCK, width), BF16),
             V((2 * BLOCK, width), BF16), V((nq, width), BF16), V((nq // 8, 2 * BLOCK), BF16), V((nq, nq), BF16),
             V((n_pass, width), BF16),
-            pltpu.SemaphoreType.DMA((72,)), pltpu.SemaphoreType.DMA((72,)),
-            pltpu.SemaphoreType.DMA((4, FAR)), pltpu.SemaphoreType.DMA((4, FAR)), pltpu.SemaphoreType.DMA((3,)),
+            pltpu.SemaphoreType.DMA((13,)), pltpu.SemaphoreType.DMA((43,)), pltpu.SemaphoreType.DMA((5,)),
         ],
         compiler_params=pltpu.CompilerParams(
             collective_id=0, has_side_effects=True, vmem_limit_bytes=58 * 1024 * 1024),
     )(query_cluster.reshape(1, nq), positive.reshape(1, nq), passage_cluster.reshape(1, n_pass), queries, passages)
+    return pl.pallas_call(
+        finish,
+        out_shape=(jax.ShapeDtypeStruct((nq, width), BF16), jax.ShapeDtypeStruct((n_pass, width), BF16)),
+        in_specs=[hbm, hbm, hbm],
+        out_specs=(hbm, hbm),
+        scratch_shapes=[V((nq, nq), BF16), V((nq, width), BF16), V((nq, width), BF16), V((n_pass, width), BF16),
+                        pltpu.SemaphoreType.DMA((4 + 2 * PARTS,))],
+        compiler_params=pltpu.CompilerParams(vmem_limit_bytes=58 * 1024 * 1024),
+    )(fsel, fg, pg)
 
 
 def solution(mesh):

time: 81.4 us -> 76.1 us (0.935)
  local copies, waits for them, and re-layouts: 3.33 us -> 0 us
  Pallas kernels: 77.3 us -> 75.3 us
    pallas_call x1, Pallas kernels: 77.3 us -> 72.2 us  [body(): pl.pallas_call(kernel, out_shape=(jax.ShapeDtypeStruct((nq, width), BF16)...]
    unnamed x4 -> x0, local copies, waits for them, and re-layouts: 3.33 us -> none
    pallas_call x0 -> x1, Pallas kernels: none -> 3.17 us  [body(): pl.pallas_call(finish, out_shape=(jax.ShapeDtypeStruct((nq, width), BF16)...]
where the time goes in v3:
time: 76.1 us; the launch traced here: 76 us
  Pallas kernels  75.3 us (99%)
    pallas_call x1, Pallas kernels, body(): pl.pallas_call(kernel, out_shape=(jax.ShapeDtypeStruct((nq, width), BF16)...  72.2 us
    pallas_call x1, Pallas kernels, body(): pl.pallas_call(finish, out_shape=(jax.ShapeDtypeStruct((nq, width), BF16)...  3.17 us

profile of v3, /device:TPU:1, one launch (start us, length us, event | category | flops | bytes accessed | tf_op | source)
XLA Modules:
  0.0 76.0 jit_solution(2763965629237395144)
XLA Ops:
  0.6 72.2 %shard_map.68 = (bf16[512,768]{1,0:T(8,128)(2,1)}, bf16[512,512]{1,0:T(8,128)(2,1)}, bf16[1024,768]{1,0:T(8,128)(2,1)}) custom-call(s32[1,512]{1,0:T(1,128)} %bitcast.4, s32[1,512]{1,0:T(1,128)} %bitcast.5, s32[1,1024]{1,0:T(1,128)} %bitcast.3, bf16[512,768]{1,0:T(8,128)(2,1)} %q_hbm.1, bf16[1024,768]{1,0:T(8,128)(2,1)} %p_hbm.1), custom_call_target="tpu_custom_call" | custom-call | tf_op jit(solution)/shard_map/pallas_call | solution.py:440
  72.8 3.2 %shard_map.69 = (bf16[512,768]{1,0:T(8,128)(2,1)}, bf16[1024,768]{1,0:T(8,128)(2,1)}) custom-call(bf16[512,512]{1,0:T(8,128)(2,1)} %get-tuple-element.5.fsel_hbm, bf16[512,768]{1,0:T(8,128)(2,1)} %get-tuple-element.6.fg_hbm, bf16[1024,768]{1,0:T(8,128)(2,1)} %get-tuple-element.7.pg_hbm), custom_call_target="tpu_custom_call" | custom-call | tf_op jit(solution)/shard_map/pallas_call | solution.py:462

commit v4 on v3

--- a/solution.py
+++ b/solution.py
@@ -66,7 +66,7 @@
 
 def kernel(qc_ref, pos_ref, pc_ref, q_hbm, p_hbm, fg_hbm, fsel_hbm, pg_hbm,
            q_ref, p_ref, p0_ref, p1_ref, pt_ref, stack, out_buf, in_buf, back_out, back_in, pack_ref, unpack_ref,
-           agb, q0_ref, prob, wt, msc, stat, stat_in, lse_ref, gt, grad, sib, comb, from_y,
+           agb, notes, spread_ref, q0_ref, prob, wt, msc, stat, stat_in, lse_ref, gt, grad, sib, comb, from_y,
            rows_ref, fg, bsel_ref, fsel_ref, pg_ref,
            ssem, rsem, lsem):
     n_pass = p_ref.shape[0]
@@ -190,6 +190,7 @@
     stores = [pltpu.make_async_copy(fsel_ref, fsel_hbm, lsem.at[4])]
     stores[0].start()
     stat[...] = jnp.zeros_like(stat)
+    spread_ref[...] = jnp.zeros_like(spread_ref)
     lse_ref[...] = jnp.zeros_like(lse_ref)
 
     def gather_start(buf, base, rows):
@@ -204,26 +205,39 @@
         on = {2: 4, 3: 5, 6: 7}[s]
         got[on] = send(blk(s), blk(on), at(dc=1), got[0])
 
+    others = pl.ds(1, 7)
+    note_row = onehot(iota((16, META), 1) == iota((16, META), 0) + 64)
+    note_group = [group(notes.at[h, others]) for h in range(2)]
+    note_come = [arrival() for h in range(2)]
     got = []
     for h in range(2):
         arrived[h]()
         rows = nn(unpack_ref[...], in_buf[h]).astype(BF16)
-        for b in range(ROW // 128):
+        note = rows[STACK - BLOCK:]
+        notes[h, 0] = nt(note_row, jnp.concatenate([note, note], axis=0)).astype(BF16)
+        for s in range(7, 0, -1):
+            send(notes.at[h, 0], notes.at[h, MIRROR[s]], at(*PLACE[s]), note_group[h], note_come[h])
+        for b in range(WIDTH // 128):
             agb[pl.ds(h * HALF, BLOCK), b * 128:(b + 1) * 128] = rows[b * BLOCK:(b + 1) * BLOCK]
         got.append(gather_start(agb, h * HALF, BLOCK))
 
-    others = pl.ds(1, 7)
     stat_group = [group(stat.at[h, others]) for h in range(2)]
     stat_come = [arrival() for h in range(2)]
     lse_group = [group(lse_ref.at[h, others]) for h in range(2)]
     lse_come = [arrival() for h in range(2)]
 
+    def unit_notes(u):
+        lower = iota((16, 128), 1) < BLOCK
+        note = [notes[u // 2, u % 2 * 4 + s].astype(F32) for s in range(4)]
+        return jnp.concatenate([jnp.where(lower, note[0], note[1]), jnp.where(lower, note[2], note[3])], axis=1)
+
     def first_pass(u):
         h, q = u // 2, u % 2
         rows = pl.ds(u * PAIR, PAIR)
         cols = pl.ds(u * PAIR, PAIR)
+        spread_ref[64:80] = unit_notes(u).astype(BF16)
         q0_ref[...] = jnp.where(iota((PAIR, 128), 1) < 64, agb[rows, 0:128].astype(F32),
-                                agb[rows, WIDTH:ROW].astype(F32)).astype(BF16)
+                                nt(eye, spread_ref[...])).astype(BF16)
         value, tops = None, []
         for m in range(5):
             left = (p0_ref[...], p1_ref[...])[m] if m < 2 else p_ref[:, CUTS[m - 1]:CUTS[m]]
@@ -268,8 +282,6 @@
             send(lse_ref.at[h, 0], lse_ref.at[h, MIRROR[s]], at(*PLACE[s]), lse_group[h], lse_come[h])
 
     base = tile * n_pass
-    pick_digit = jnp.where(iota((8, META), 1) == 69, 64.0,
-                           jnp.where(iota((8, META), 1) == 70, 1.0, 0.0)).astype(BF16)
 
     def second_pass(u, between=None):
         h, q = u // 2, u % 2
@@ -277,7 +289,8 @@
         cols = pl.ds(u * PAIR, PAIR)
         if q == 1:
             remote(lse_ref.at[h, others], lse_ref.at[h, others], lse_group[h], lse_come[h], at(dc=1)).wait_recv()
-        goal = nt(pick_digit, agb[rows, WIDTH:ROW])[0:1].astype(I32) - base
+        note = unit_notes(u)
+        goal = (note[5:6] * 64.0 + note[6:7]).astype(I32) - base
         lower = iota((8, 128), 1) < BLOCK
         lse = jnp.concatenate([jnp.where(lower, lse_ref[h, 4 * q + s], lse_ref[h, 4 * q + s + 1]) for s in (0, 2)],
                               axis=1)
@@ -344,6 +357,7 @@
         return store
 
     def gather_near(h):
+        remote(notes.at[h, others], notes.at[h, others], note_group[h], note_come[h], at(dc=1)).wait_recv()
         gather_pass(agb, h * HALF, BLOCK, got[h], 2)
         gather_pass(agb, h * HALF, BLOCK, got[h], 3)
         got[h][1].wait_recv()
@@ -447,14 +461,14 @@
             V((nq, width), BF16),
             V((n_pass, width), BF16), V((n_pass, 128), BF16), V((n_pass, 128), BF16), V((width, n_pass), BF16),
             V((STACK, 128), BF16), *[V((2, HALF, 128), BF16)] * 4, V((HALF, STACK), BF16), V((STACK, HALF), BF16),
-            V((SLOTS, ROW), BF16), V((PAIR, 128), BF16),
+            V((SLOTS, width), BF16), V((2, 8, 16, 128), BF16), V((META, PAIR), BF16), V((PAIR, 128), BF16),
             V((5, n_pass, SLOTS), F32), V((5, n_pass, SLOTS), BF16), V((8, SLOTS), F32),
             V((2, 8, 8, 128), F32), V((2, 8, 8, 128), F32), V((2, 8, 8, 128), F32),
             V((width, PAIR), BF16), V((SLOTS, width), BF16),
             V((2, 4, BLOCK, width), BF16), V((2, 4, BLOCK, width), BF16), V((2, 4, BLOCK, width), BF16),
             V((2 * BLOCK, width), BF16), V((nq, width), BF16), V((nq // 8, 2 * BLOCK), BF16), V((nq, nq), BF16),
             V((n_pass, width), BF16),
-            pltpu.SemaphoreType.DMA((13,)), pltpu.SemaphoreType.DMA((43,)), pltpu.SemaphoreType.DMA((5,)),
+            pltpu.SemaphoreType.DMA((15,)), pltpu.SemaphoreType.DMA((45,)), pltpu.SemaphoreType.DMA((5,)),
         ],
         compiler_params=pltpu.CompilerParams(
             collective_id=0, has_side_effects=True, vmem_limit_bytes=58 * 1024 * 1024),

time: 76.1 us -> 76.1 us (level)
  no operation moved by 1% of the time
where the time goes in v4:
time: 76.1 us; the launch traced here: 76 us
  Pallas kernels  75.3 us (99%)
    pallas_call x1, Pallas kernels, body(): pl.pallas_call(kernel, out_shape=(jax.ShapeDtypeStruct((nq, width), BF16)...  72.1 us
    pallas_call x1, Pallas kernels, body(): pl.pallas_call(finish, out_shape=(jax.ShapeDtypeStruct((nq, width), BF16)...  3.17 us

profile of v4, /device:TPU:1, one launch (start us, length us, event | category | flops | bytes accessed | tf_op | source)
XLA Modules:
  0.0 76.0 jit_solution(700908086215701719)
XLA Ops:
  0.6 72.1 %shard_map.68 = (bf16[512,768]{1,0:T(8,128)(2,1)}, bf16[512,512]{1,0:T(8,128)(2,1)}, bf16[1024,768]{1,0:T(8,128)(2,1)}) custom-call(s32[1,512]{1,0:T(1,128)} %bitcast.4, s32[1,512]{1,0:T(1,128)} %bitcast.5, s32[1,1024]{1,0:T(1,128)} %bitcast.3, bf16[512,768]{1,0:T(8,128)(2,1)} %q_hbm.1, bf16[1024,768]{1,0:T(8,128)(2,1)} %p_hbm.1), custom_call_target="tpu_custom_call" | custom-call | tf_op jit(solution)/shard_map/pallas_call | solution.py:454
  72.8 3.2 %shard_map.69 = (bf16[512,768]{1,0:T(8,128)(2,1)}, bf16[1024,768]{1,0:T(8,128)(2,1)}) custom-call(bf16[512,512]{1,0:T(8,128)(2,1)} %get-tuple-element.5.fsel_hbm, bf16[512,768]{1,0:T(8,128)(2,1)} %get-tuple-element.6.fg_hbm, bf16[1024,768]{1,0:T(8,128)(2,1)} %get-tuple-element.7.pg_hbm), custom_call_target="tpu_custom_call" | custom-call | tf_op jit(solution)/shard_map/pallas_call | solution.py:476

commit v5 on v3

--- a/solution.py
+++ b/solution.py
@@ -31,7 +31,7 @@
 STACK = ROW // 128 * BLOCK
 
 PLACE = ((0, 0), (0, 1), (1, 0), (3, 0), (1, 1), (3, 1), (2, 0), (2, 1))
-MIRROR = tuple(PLACE.index(((NY - dy) % NY, dc)) for dy, dc in PLACE)
+CHIPS = (0, 1, 3, 2)
 MESH = pl.DeviceIdType.MESH
 PARTS = 4
 
@@ -66,7 +66,7 @@
 
 def kernel(qc_ref, pos_ref, pc_ref, q_hbm, p_hbm, fg_hbm, fsel_hbm, pg_hbm,
            q_ref, p_ref, p0_ref, p1_ref, pt_ref, stack, out_buf, in_buf, back_out, back_in, pack_ref, unpack_ref,
-           agb, q0_ref, prob, wt, msc, stat, stat_in, lse_ref, gt, grad, sib, comb, from_y,
+           agb, q0_ref, prob, wt, msc, stat, core_out, core_in, chip_out, chip_in, lse_ref, gt, grad, sib, comb, from_y,
            rows_ref, fg, bsel_ref, fsel_ref, pg_ref,
            ssem, rsem, lsem):
     n_pass = p_ref.shape[0]
@@ -78,11 +78,15 @@
     def at(dy=0, dc=0):
         return (dp, lax.rem(y + dy, NY) * NC + lax.rem(core + dc, NC))
 
-    def ahead(i):
-        return (lax.rem(x + lax.div(i, NZ), NX) * NZ + lax.rem(z + lax.rem(i, NZ), NZ), tile)
-
-    def behind(i):
-        return (lax.rem(x + NX - lax.div(i, NZ), NX) * NZ + lax.rem(z + NZ - lax.rem(i, NZ), NZ), tile)
+    places = sorted(((dx, dz) for dx in range(NX) for dz in range(NZ) if dx or dz), key=lambda d: abs(d[1] - NZ // 2))
+    x_at = [lax.rem(x + d, NX) * NZ for d in range(NX)]
+    z_at = [lax.rem(z + d, NZ) for d in range(NZ)]
+
+    def ahead(dx, dz):
+        return (x_at[dx] + z_at[dz], tile)
+
+    def behind(dx, dz):
+        return ahead((NX - dx) % NX, (NZ - dz) % NZ)
 
     groups, received = [], []
 
@@ -107,19 +111,15 @@
         rest = pl.ds(CHUNK, (FAR - 1) * CHUNK)
         g, n = group(src.at[rest]), arrival()
 
-        def go(i, carry):
-            rows = pl.ds(pl.multiple_of(i * CHUNK, CHUNK), CHUNK)
-            remote(src.at[rows], dst.at[rows], g, n, where(i)).start()
-            return carry
-
-        lax.fori_loop(1, FAR, go, 0)
+        for dx, dz in places:
+            rows = pl.ds((dx * NZ + dz) * CHUNK, CHUNK)
+            remote(src.at[rows], dst.at[rows], g, n, where(dx, dz)).start()
         dst[pl.ds(0, CHUNK)] = src[pl.ds(0, CHUNK)]
-        return remote(src.at[rest], dst.at[rest], g, n, where(1)).wait_recv
+        return remote(src.at[rest], dst.at[rest], g, n, at(dc=1)).wait_recv
 
     barrier = pltpu.get_barrier_semaphore()
-    for dx, dz in sorted(((i // NZ, i % NZ) for i in range(1, FAR)), key=lambda d: abs(d[1] - NZ // 2)):
-        there = lax.rem(x + dx, NX) * NZ + lax.rem(z + dz, NZ)
-        pl.semaphore_signal(barrier, inc=1, device_id=(there, tile), device_id_type=MESH)
+    for dx, dz in places:
+        pl.semaphore_signal(barrier, inc=1, device_id=ahead(dx, dz), device_id_type=MESH)
     for dy, dc in PLACE[1:]:
         pl.semaphore_signal(barrier, inc=1, device_id=at(dy, dc), device_id_type=MESH)
     load_q = pltpu.make_async_copy(q_hbm, q_ref, lsem.at[3])
@@ -190,7 +190,6 @@
     stores = [pltpu.make_async_copy(fsel_ref, fsel_hbm, lsem.at[4])]
     stores[0].start()
     stat[...] = jnp.zeros_like(stat)
-    lse_ref[...] = jnp.zeros_like(lse_ref)
 
     def gather_start(buf, base, rows):
         blk = lambda s: buf.at[pl.ds(base + s * rows, rows)]
@@ -212,11 +211,10 @@
             agb[pl.ds(h * HALF, BLOCK), b * 128:(b + 1) * 128] = rows[b * BLOCK:(b + 1) * BLOCK]
         got.append(gather_start(agb, h * HALF, BLOCK))
 
-    others = pl.ds(1, 7)
-    stat_group = [group(stat.at[h, others]) for h in range(2)]
-    stat_come = [arrival() for h in range(2)]
-    lse_group = [group(lse_ref.at[h, others]) for h in range(2)]
-    lse_come = [arrival() for h in range(2)]
+    core_group = [group(core_out.at[h]) for h in range(2)]
+    core_come = [arrival() for h in range(2)]
+    chip_group = [group(chip_in.at[h]) for h in range(2)]
+    chip_come = [arrival() for h in range(2)]
 
     def first_pass(u):
         h, q = u // 2, u % 2
@@ -249,23 +247,45 @@
             total = jnp.sum(sums[m], axis=0, keepdims=True)
             msc[m:m + 1, cols] = top
             lse = top + jnp.log(total)
-            for s in range(4):
-                stat[h, 4 * q + s, m:m + 1] = lse[:, s // 2 * 128:s // 2 * 128 + 128]
-        for s in range(4 * q, 4 * q + 4):
-            if s:
-                send(stat.at[h, s], stat_in.at[h, MIRROR[s]], at(*PLACE[s]), stat_group[h], stat_come[h])
+            for t in range(2):
+                stat[h, 2 * q + t, m:m + 1] = lse[:, t * 128:(t + 1) * 128]
+
+    lower = iota((8, 128), 1) < BLOCK
+
+    def turn(value):
+        return pltpu.roll(value, BLOCK, 1)
+
+    def by_chip(a, b):
+        return jnp.where(lower, a, turn(b)), jnp.where(lower, turn(a), b)
+
+    def join(values):
+        top = functools.reduce(jnp.maximum, values)
+        return top + jnp.log(functools.reduce(jnp.add, [jnp.exp(v - top) for v in values]))
+
+    def totals_to_core(h):
+        core_out[h, 0] = stat[h, 0]
+        core_out[h, 1], core_out[h, 2] = by_chip(stat[h, 1], stat[h, 2])
+        core_out[h, 3] = stat[h, 3]
+        send(core_out.at[h], core_in.at[h], at(dc=1), core_group[h], core_come[h])
+
+    def totals_to_chips(h):
+        remote(core_out.at[h], core_in.at[h], core_group[h], core_come[h], at(dc=1)).wait_recv()
+        for t in range(4):
+            chip_out[h, t] = join([core_out[h, t], turn(core_in[h, t])])
+        for t in (3, 1, 2):
+            send(chip_out.at[h], chip_in.at[h, t - 1], at(dy=CHIPS[t]), chip_group[h], chip_come[h])
 
     def totals(h):
-        parts = [stat[h, 0]]
-        remote(stat.at[h, others], stat_in.at[h, others], stat_group[h], stat_come[h], at(dc=1)).wait_recv()
-        for s in range(1, 8):
-            value = stat_in[h, MIRROR[s]]
-            parts.append(pltpu.roll(value, BLOCK, 1) if s % 2 else value)
-        top = functools.reduce(jnp.maximum, parts)
-        lse = top + jnp.log(functools.reduce(jnp.add, [jnp.exp(v - top) for v in parts]))
-        lse_ref[h, 0] = jnp.where(iota((8, 128), 1) < BLOCK, lse, pltpu.roll(lse, BLOCK, 1))
-        for s in range(7, 0, -1):
-            send(lse_ref.at[h, 0], lse_ref.at[h, MIRROR[s]], at(*PLACE[s]), lse_group[h], lse_come[h])
+        remote(chip_in.at[h], chip_in.at[h], chip_group[h], chip_come[h], at(dc=1)).wait_recv()
+        tiles = []
+        for t in range(4):
+            values = [chip_out[h, t]]
+            for f in (1, 2, 3):
+                values.append(chip_in[h, f - 1, CHIPS.index((CHIPS[t] + CHIPS[f]) % NY)])
+            tiles.append(join(values))
+        lse_ref[h, 0] = tiles[0]
+        lse_ref[h, 1], lse_ref[h, 2] = by_chip(tiles[1], tiles[2])
+        lse_ref[h, 3] = tiles[3]
 
     base = tile * n_pass
     pick_digit = jnp.where(iota((8, META), 1) == 69, 64.0,
@@ -275,12 +295,8 @@
         h, q = u // 2, u % 2
         rows = pl.ds(u * PAIR, PAIR)
         cols = pl.ds(u * PAIR, PAIR)
-        if q == 1:
-            remote(lse_ref.at[h, others], lse_ref.at[h, others], lse_group[h], lse_come[h], at(dc=1)).wait_recv()
         goal = nt(pick_digit, agb[rows, WIDTH:ROW])[0:1].astype(I32) - base
-        lower = iota((8, 128), 1) < BLOCK
-        lse = jnp.concatenate([jnp.where(lower, lse_ref[h, 4 * q + s], lse_ref[h, 4 * q + s + 1]) for s in (0, 2)],
-                              axis=1)
+        lse = jnp.concatenate([lse_ref[h, 2 * q], lse_ref[h, 2 * q + 1]], axis=1)
         factor = [jnp.exp(msc[m:m + 1, cols] - lse[m:m + 1]) * SCALES[m] for m in range(5)]
         small = 64
 
@@ -357,20 +373,24 @@
     first_pass(0)
     gather_rest(0)
     first_pass(1)
+    totals_to_core(0)
     gather_near(1)
     first_pass(2)
-    totals(0)
+    totals_to_chips(0)
     gather_rest(1)
     first_pass(3)
+    totals_to_core(1)
+    totals(0)
+    totals_to_chips(1)
 
     second_pass(1)
     for s in (7, 4, 5):
         to_core(0, s)
-    totals(1)
     second_pass(0, lambda: to_chip(0, 6))
     to_core(0, 1)
     to_chip(0, 2)
     to_chip(0, 3)
+    totals(1)
     second_pass(3)
     for s in (7, 4, 5):
         to_core(1, s)
@@ -449,7 +469,7 @@
             V((STACK, 128), BF16), *[V((2, HALF, 128), BF16)] * 4, V((HALF, STACK), BF16), V((STACK, HALF), BF16),
             V((SLOTS, ROW), BF16), V((PAIR, 128), BF16),
             V((5, n_pass, SLOTS), F32), V((5, n_pass, SLOTS), BF16), V((8, SLOTS), F32),
-            V((2, 8, 8, 128), F32), V((2, 8, 8, 128), F32), V((2, 8, 8, 128), F32),
+            *[V((2, 4, 8, 128), F32)] * 4, V((2, 3, 4, 8, 128), F32), V((2, 4, 8, 128), F32),
             V((width, PAIR), BF16), V((SLOTS, width), BF16),
             V((2, 4, BLOCK, width), BF16), V((2, 4, BLOCK, width), BF16), V((2, 4, BLOCK, width), BF16),
             V((2 * BLOCK, width), BF16), V((nq, width), BF16), V((nq // 8, 2 * BLOCK), BF16), V((nq, nq), BF16),

time: 76.1 us -> 72.6 us (0.954)
  Pallas kernels: 75.3 us -> 71.6 us
    pallas_call x1, Pallas kernels: 72.2 us -> 68.4 us  [body(): pl.pallas_call(kernel, out_shape=(jax.ShapeDtypeStruct((nq, width), BF16)...]
where the time goes in v5:
time: 72.6 us; the launch traced here: 72.4 us
  Pallas kernels  71.6 us (99%)
  between operations  0.8 us (1%)
    pallas_call x1, Pallas kernels, body(): pl.pallas_call(kernel, out_shape=(jax.ShapeDtypeStruct((nq, width), BF16)...  68.4 us
    pallas_call x1, Pallas kernels, body(): pl.pallas_call(finish, out_shape=(jax.ShapeDtypeStruct((nq, width), BF16)...  3.17 us

profile of v5, /device:TPU:1, one launch (start us, length us, event | category | flops | bytes accessed | tf_op | source)
XLA Modules:
  0.0 72.4 jit_solution(479919675399375114)
XLA Ops:
  0.6 68.4 %shard_map.68 = (bf16[512,768]{1,0:T(8,128)(2,1)}, bf16[512,512]{1,0:T(8,128)(2,1)}, bf16[1024,768]{1,0:T(8,128)(2,1)}) custom-call(s32[1,512]{1,0:T(1,128)} %bitcast.4, s32[1,512]{1,0:T(1,128)} %bitcast.5, s32[1,1024]{1,0:T(1,128)} %bitcast.3, bf16[512,768]{1,0:T(8,128)(2,1)} %q_hbm.1, bf16[1024,768]{1,0:T(8,128)(2,1)} %p_hbm.1), custom_call_target="tpu_custom_call" | custom-call | tf_op jit(solution)/shard_map/pallas_call | solution.py:460
  69.1 3.2 %shard_map.69 = (bf16[512,768]{1,0:T(8,128)(2,1)}, bf16[1024,768]{1,0:T(8,128)(2,1)}) custom-call(bf16[512,512]{1,0:T(8,128)(2,1)} %get-tuple-element.5.fsel_hbm, bf16[512,768]{1,0:T(8,128)(2,1)} %get-tuple-element.6.fg_hbm, bf16[1024,768]{1,0:T(8,128)(2,1)} %get-tuple-element.7.pg_hbm), custom_call_target="tpu_custom_call" | custom-call | tf_op jit(solution)/shard_map/pallas_call | solution.py:482

commit v6 on v5

--- a/solution.py
+++ b/solution.py
@@ -120,7 +120,8 @@
     barrier = pltpu.get_barrier_semaphore()
     for dx, dz in places:
         pl.semaphore_signal(barrier, inc=1, device_id=ahead(dx, dz), device_id_type=MESH)
-    for dy, dc in PLACE[1:]:
+    near_by = [(0, 1), (1, 0), (2, 0), (3, 0)]
+    for dy, dc in near_by:
         pl.semaphore_signal(barrier, inc=1, device_id=at(dy, dc), device_id_type=MESH)
     load_q = pltpu.make_async_copy(q_hbm, q_ref, lsem.at[3])
     load_q.start()
@@ -164,7 +165,7 @@
         stack[pl.ds(STACK - BLOCK, BLOCK)] = meta[h * BLOCK:(h + 1) * BLOCK]
         out_buf[h] = nn(pack_ref[...], stack[...]).astype(BF16)
 
-    pl.semaphore_wait(barrier, FAR - 1 + 7)
+    pl.semaphore_wait(barrier, len(places) + len(near_by))
 
     arrived = [exchange(out_buf.at[h], in_buf.at[h], ahead) for h in range(2)]
 
@@ -381,9 +382,8 @@
     first_pass(3)
     totals_to_core(1)
     totals(0)
-    totals_to_chips(1)
-
-    second_pass(1)
+
+    second_pass(1, lambda: totals_to_chips(1))
     for s in (7, 4, 5):
         to_core(0, s)
     second_pass(0, lambda: to_chip(0, 6))
@@ -411,14 +411,24 @@
             rows_ref[pl.ds(h * BLOCK, BLOCK), b * 128:(b + 1) * 128] = rows[b * BLOCK:(b + 1) * BLOCK]
     fg[pl.ds(0, lines)] = nn(bsel_ref[...], rows_ref[...]).astype(BF16)
     last = gather_start(fg, 0, lines)
-    for s in (2, 3, 6):
-        gather_pass(fg, 0, lines, last, s)
-    for s in (1, 4, 5, 7):
-        last[s].wait_recv()
+
+    def write_out(s):
+        rows = pl.ds(s * lines, 2 * lines)
+        stores.append(pltpu.make_async_copy(fg.at[rows], fg_hbm.at[rows], lsem.at[5 + s // 2]))
+        stores[-1].start()
+
+    last[1].wait_recv()
+    write_out(0)
+    gather_pass(fg, 0, lines, last, 2)
+    gather_pass(fg, 0, lines, last, 3)
+    write_out(2)
+    last[4].wait_recv()
+    last[5].wait_recv()
+    write_out(4)
+    gather_pass(fg, 0, lines, last, 6)
+    last[7].wait_recv()
+    write_out(6)
     assert len(groups) == ssem.shape[0] and len(received) == rsem.shape[0]
-    write = pltpu.make_async_copy(fg, fg_hbm, lsem.at[3])
-    write.start()
-    write.wait()
     for store in stores:
         store.wait()
     for g, all_sent in enumerate(groups):
@@ -474,7 +484,7 @@
             V((2, 4, BLOCK, width), BF16), V((2, 4, BLOCK, width), BF16), V((2, 4, BLOCK, width), BF16),
             V((2 * BLOCK, width), BF16), V((nq, width), BF16), V((nq // 8, 2 * BLOCK), BF16), V((nq, nq), BF16),
             V((n_pass, width), BF16),
-            pltpu.SemaphoreType.DMA((13,)), pltpu.SemaphoreType.DMA((43,)), pltpu.SemaphoreType.DMA((5,)),
+            pltpu.SemaphoreType.DMA((13,)), pltpu.SemaphoreType.DMA((43,)), pltpu.SemaphoreType.DMA((9,)),
         ],
         compiler_params=pltpu.CompilerParams(
             collective_id=0, has_side_effects=True, vmem_limit_bytes=58 * 1024 * 1024),

time: 72.6 us -> 70.8 us (0.975)
  Pallas kernels: 71.6 us -> 69.8 us
    pallas_call x1, Pallas kernels: 68.4 us -> 66.7 us  [body(): pl.pallas_call(kernel, out_shape=(jax.ShapeDtypeStruct((nq, width), BF16)...]
where the time goes in v6:
time: 70.8 us; the launch traced here: 70.6 us
  Pallas kernels  69.8 us (99%)
  between operations  0.8 us (1%)
    pallas_call x1, Pallas kernels, body(): pl.pallas_call(kernel, out_shape=(jax.ShapeDtypeStruct((nq, width), BF16)...  66.7 us
    pallas_call x1, Pallas kernels, body(): pl.pallas_call(finish, out_shape=(jax.ShapeDtypeStruct((nq, width), BF16)...  3.17 us

profile of v6, /device:TPU:1, one launch (start us, length us, event | category | flops | bytes accessed | tf_op | source)
XLA Modules:
  0.0 70.6 jit_solution(2373183775490845651)
XLA Ops:
  0.6 66.7 %shard_map.68 = (bf16[512,768]{1,0:T(8,128)(2,1)}, bf16[512,512]{1,0:T(8,128)(2,1)}, bf16[1024,768]{1,0:T(8,128)(2,1)}) custom-call(s32[1,512]{1,0:T(1,128)} %bitcast.4, s32[1,512]{1,0:T(1,128)} %bitcast.5, s32[1,1024]{1,0:T(1,128)} %bitcast.3, bf16[512,768]{1,0:T(8,128)(2,1)} %q_hbm.1, bf16[1024,768]{1,0:T(8,128)(2,1)} %p_hbm.1), custom_call_target="tpu_custom_call" | custom-call | tf_op jit(solution)/shard_map/pallas_call | solution.py:470
  67.3 3.2 %shard_map.69 = (bf16[512,768]{1,0:T(8,128)(2,1)}, bf16[1024,768]{1,0:T(8,128)(2,1)}) custom-call(bf16[512,512]{1,0:T(8,128)(2,1)} %get-tuple-element.5.fsel_hbm, bf16[512,768]{1,0:T(8,128)(2,1)} %get-tuple-element.6.fg_hbm, bf16[1024,768]{1,0:T(8,128)(2,1)} %get-tuple-element.7.pg_hbm), custom_call_target="tpu_custom_call" | custom-call | tf_op jit(solution)/shard_map/pallas_call | solution.py:492

commit v7 on v6

--- a/solution.py
+++ b/solution.py
@@ -64,8 +64,8 @@
     return lax.shift_right_logical(a, n)
 
 
-def kernel(qc_ref, pos_ref, pc_ref, q_hbm, p_hbm, fg_hbm, fsel_hbm, pg_hbm,
-           q_ref, p_ref, p0_ref, p1_ref, pt_ref, stack, out_buf, in_buf, back_out, back_in, pack_ref, unpack_ref,
+def kernel(qc_hbm, pos_hbm, pc_hbm, q_hbm, p_hbm, fg_hbm, fsel_hbm, pg_hbm,
+           qc_ref, pos_ref, pc_ref, q_ref, p_ref, p0_ref, p1_ref, pt_ref, stack, out_buf, in_buf, back_out, back_in, pack_ref, unpack_ref,
            agb, q0_ref, prob, wt, msc, stat, core_out, core_in, chip_out, chip_in, lse_ref, gt, grad, sib, comb, from_y,
            rows_ref, fg, bsel_ref, fsel_ref, pg_ref,
            ssem, rsem, lsem):
@@ -123,12 +123,18 @@
     near_by = [(0, 1), (1, 0), (2, 0), (3, 0)]
     for dy, dc in near_by:
         pl.semaphore_signal(barrier, inc=1, device_id=at(dy, dc), device_id_type=MESH)
+    small_loads = [pltpu.make_async_copy(src, dst, lsem.at[9 + i]) for i, (src, dst) in
+                   enumerate(((qc_hbm, qc_ref), (pos_hbm, pos_ref), (pc_hbm, pc_ref)))]
+    for load in small_loads:
+        load.start()
     load_q = pltpu.make_async_copy(q_hbm, q_ref, lsem.at[3])
     load_q.start()
     load_p = pltpu.make_async_copy(p_hbm, p_ref, lsem.at[0])
     load_p.start()
 
     nq = q_ref.shape[0]
+    for load in small_loads:
+        load.wait()
     cluster = qc_ref[...]
     owner = shift(cluster, 2)
     local = lax.bitwise_and(cluster, 3)
@@ -156,9 +162,6 @@
     r, c = iota((HALF, STACK), 0), iota((HALF, STACK), 1)
     pack_ref[...] = onehot((shift(lax.bitwise_and(r, CHUNK - 1), 1) == shift(c, 6))
                            & (lax.bitwise_and(c, BLOCK - 1) == shift(r, 4) * 2 + lax.bitwise_and(r, 1)))
-    c, r = iota((STACK, HALF), 0), iota((STACK, HALF), 1)
-    unpack_ref[...] = onehot((shift(lax.bitwise_and(r, CHUNK - 1), 1) == shift(c, 6))
-                             & (lax.bitwise_and(c, BLOCK - 1) == shift(r, 4) * 2 + lax.bitwise_and(r, 1)))
     for h in range(2):
         for b in range(WIDTH // 128):
             stack[pl.ds(b * BLOCK, BLOCK)] = sent[h * BLOCK:(h + 1) * BLOCK, b * 128:(b + 1) * 128]
@@ -169,6 +172,9 @@
 
     arrived = [exchange(out_buf.at[h], in_buf.at[h], ahead) for h in range(2)]
 
+    c, r = iota((STACK, HALF), 0), iota((STACK, HALF), 1)
+    unpack_ref[...] = onehot((shift(lax.bitwise_and(r, CHUNK - 1), 1) == shift(c, 6))
+                             & (lax.bitwise_and(c, BLOCK - 1) == shift(r, 4) * 2 + lax.bitwise_and(r, 1)))
     clusters = pc_ref[...]
     lane_row = iota((META, n_pass), 0)
     off = jnp.where((lane_row == clusters - CL_OWN * dp + 64) | (lane_row > 68) | (lane_row < 64), 0.0, NEGATIVE)
@@ -464,17 +470,16 @@
 def body(queries, passages, query_cluster, passage_cluster, positive):
     nq, width = queries.shape
     n_pass = passages.shape[0]
-    vmem = pl.BlockSpec(memory_space=pltpu.VMEM)
     hbm = pl.BlockSpec(memory_space=pl.ANY)
     V = pltpu.VMEM
     fg, fsel, pg = pl.pallas_call(
         kernel,
         out_shape=(jax.ShapeDtypeStruct((nq, width), BF16), jax.ShapeDtypeStruct((nq, nq), BF16),
                    jax.ShapeDtypeStruct((n_pass, width), BF16)),
-        in_specs=[vmem, vmem, vmem, hbm, hbm],
+        in_specs=[hbm] * 5,
         out_specs=(hbm, hbm, hbm),
         scratch_shapes=[
-            V((nq, width), BF16),
+            V((1, nq), I32), V((1, nq), I32), V((1, n_pass), I32), V((nq, width), BF16),
             V((n_pass, width), BF16), V((n_pass, 128), BF16), V((n_pass, 128), BF16), V((width, n_pass), BF16),
             V((STACK, 128), BF16), *[V((2, HALF, 128), BF16)] * 4, V((HALF, STACK), BF16), V((STACK, HALF), BF16),
             V((SLOTS, ROW), BF16), V((PAIR, 128), BF16),
@@ -484,7 +489,7 @@
             V((2, 4, BLOCK, width), BF16), V((2, 4, BLOCK, width), BF16), V((2, 4, BLOCK, width), BF16),
             V((2 * BLOCK, width), BF16), V((nq, width), BF16), V((nq // 8, 2 * BLOCK), BF16), V((nq, nq), BF16),
             V((n_pass, width), BF16),
-            pltpu.SemaphoreType.DMA((13,)), pltpu.SemaphoreType.DMA((43,)), pltpu.SemaphoreType.DMA((9,)),
+            pltpu.SemaphoreType.DMA((13,)), pltpu.SemaphoreType.DMA((43,)), pltpu.SemaphoreType.DMA((12,)),
         ],
         compiler_params=pltpu.CompilerParams(
             collective_id=0, has_side_effects=True, vmem_limit_bytes=58 * 1024 * 1024),

time: 70.8 us -> 70.9 us (level)
  no operation moved by 1% of the time
where the time goes in v7:
time: 70.9 us; the launch traced here: 70.8 us
  Pallas kernels  70 us (99%)
  between operations  0.8 us (1%)
    pallas_call x1, Pallas kernels, body(): pl.pallas_call(kernel, out_shape=(jax.ShapeDtypeStruct((nq, width), BF16)...  66.8 us
    pallas_call x1, Pallas kernels, body(): pl.pallas_call(finish, out_shape=(jax.ShapeDtypeStruct((nq, width), BF16)...  3.17 us

profile of v7, /device:TPU:1, one launch (start us, length us, event | category | flops | bytes accessed | tf_op | source)
XLA Modules:
  0.0 70.8 jit_solution(12775654328531211446)
XLA Ops:
  0.6 66.8 %shard_map.68 = (bf16[512,768]{1,0:T(8,128)(2,1)}, bf16[512,512]{1,0:T(8,128)(2,1)}, bf16[1024,768]{1,0:T(8,128)(2,1)}) custom-call(s32[1,512]{1,0:T(1,128)} %bitcast.4, s32[1,512]{1,0:T(1,128)} %bitcast.5, s32[1,1024]{1,0:T(1,128)} %bitcast.3, bf16[512,768]{1,0:T(8,128)(2,1)} %q_hbm.1, bf16[1024,768]{1,0:T(8,128)(2,1)} %p_hbm.1), custom_call_target="tpu_custom_call" | custom-call | tf_op jit(solution)/shard_map/pallas_call | solution.py:475
  67.4 3.2 %shard_map.69 = (bf16[512,768]{1,0:T(8,128)(2,1)}, bf16[1024,768]{1,0:T(8,128)(2,1)}) custom-call(bf16[512,512]{1,0:T(8,128)(2,1)} %get-tuple-element.5.fsel_hbm, bf16[512,768]{1,0:T(8,128)(2,1)} %get-tuple-element.6.fg_hbm, bf16[1024,768]{1,0:T(8,128)(2,1)} %get-tuple-element.7.pg_hbm), custom_call_target="tpu_custom_call" | custom-call | tf_op jit(solution)/shard_map/pallas_call | solution.py:497

commit v8 on v6

--- a/solution.py
+++ b/solution.py
@@ -292,7 +292,7 @@
     pick_digit = jnp.where(iota((8, META), 1) == 69, 64.0,
                            jnp.where(iota((8, META), 1) == 70, 1.0, 0.0)).astype(BF16)
 
-    def second_pass(u, between=None):
+    def second_pass(u, between=None, after_upper=None):
         h, q = u // 2, u % 2
         rows = pl.ds(u * PAIR, PAIR)
         cols = pl.ds(u * PAIR, PAIR)
@@ -315,10 +315,15 @@
         lax.fori_loop(0, n_pass // small, weigh, 0)
         if between is not None:
             between()
-        for m in range(5):
-            lo = CUTS[m - 1] if m else 0
-            gt[lo:CUTS[m]] = nn(pt_ref[lo:CUTS[m]], wt[m, :, cols]).astype(BF16)
-        grad[rows] = nt(eye, gt[...]).astype(BF16)
+        width = PAIR if after_upper is None else PAIR // 2
+        for start in range(PAIR - width, -1, -width):
+            part = slice(start, start + width)
+            for m in range(5):
+                lo = CUTS[m - 1] if m else 0
+                gt[lo:CUTS[m], part] = nn(pt_ref[lo:CUTS[m]], wt[m, :, u * PAIR + start:u * PAIR + start + width]).astype(BF16)
+            grad[pl.ds(u * PAIR + start, width)] = nt(eye[:width, :width], gt[:, part]).astype(BF16)
+            if start:
+                after_upper()
 
     sums_in = {}
     sum_group = [group(grad.at[pl.ds(h * HALF, 7 * BLOCK)]) for h in range(2)]
@@ -386,18 +391,14 @@
     second_pass(1, lambda: totals_to_chips(1))
     for s in (7, 4, 5):
         to_core(0, s)
-    second_pass(0, lambda: to_chip(0, 6))
+    second_pass(0, lambda: to_chip(0, 6), lambda: (to_chip(0, 2), to_chip(0, 3)))
     to_core(0, 1)
-    to_chip(0, 2)
-    to_chip(0, 3)
     totals(1)
     second_pass(3)
     for s in (7, 4, 5):
         to_core(1, s)
-    second_pass(2, lambda: to_chip(1, 6))
+    second_pass(2, lambda: to_chip(1, 6), lambda: (to_chip(1, 2), to_chip(1, 3)))
     to_core(1, 1)
-    to_chip(1, 2)
-    to_chip(1, 3)
     home = [go_back(0)]
     stores.append(passage_part(0))
     home.append(go_back(1))

time: 70.8 us -> 72.3 us (1.021)
  Pallas kernels: 69.8 us -> 71.3 us
    pallas_call x1, Pallas kernels: 66.7 us -> 68.1 us  [body(): pl.pallas_call(kernel, out_shape=(jax.ShapeDtypeStruct((nq, width), BF16)...]
where the time goes in v8:
time: 72.3 us; the launch traced here: 72.1 us
  Pallas kernels  71.3 us (99%)
  between operations  0.8 us (1%)
    pallas_call x1, Pallas kernels, body(): pl.pallas_call(kernel, out_shape=(jax.ShapeDtypeStruct((nq, width), BF16)...  68.1 us
    pallas_call x1, Pallas kernels, body(): pl.pallas_call(finish, out_shape=(jax.ShapeDtypeStruct((nq, width), BF16)...  3.17 us

profile of v8, /device:TPU:1, one launch (start us, length us, event | category | flops | bytes accessed | tf_op | source)
XLA Modules:
  0.0 72.1 jit_solution(4536367138290511504)
XLA Ops:
  0.6 68.1 %shard_map.68 = (bf16[512,768]{1,0:T(8,128)(2,1)}, bf16[512,512]{1,0:T(8,128)(2,1)}, bf16[1024,768]{1,0:T(8,128)(2,1)}) custom-call(s32[1,512]{1,0:T(1,128)} %bitcast.4, s32[1,512]{1,0:T(1,128)} %bitcast.5, s32[1,1024]{1,0:T(1,128)} %bitcast.3, bf16[512,768]{1,0:T(8,128)(2,1)} %q_hbm.1, bf16[1024,768]{1,0:T(8,128)(2,1)} %p_hbm.1), custom_call_target="tpu_custom_call" | custom-call | tf_op jit(solution)/shard_map/pallas_call | solution.py:471
  68.8 3.2 %shard_map.69 = (bf16[512,768]{1,0:T(8,128)(2,1)}, bf16[1024,768]{1,0:T(8,128)(2,1)}) custom-call(bf16[512,512]{1,0:T(8,128)(2,1)} %get-tuple-element.5.fsel_hbm, bf16[512,768]{1,0:T(8,128)(2,1)} %get-tuple-element.6.fg_hbm, bf16[1024,768]{1,0:T(8,128)(2,1)} %get-tuple-element.7.pg_hbm), custom_call_target="tpu_custom_call" | custom-call | tf_op jit(solution)/shard_map/pallas_call | solution.py:493
